TPU v7x, 512 devices: a whole 4x4x16 slice. The times are simulated.
512 devices in a mesh: row: 32 (over x_hi, z), col: 16 (over x_lo, y, core).
Axes of the slice: x: 4 (x_hi: 2, x_lo: 2; x = x_hi * 2 + x_lo), y: 4, z: 16, core: 2. Of those that a mesh axis runs over, the one named last changes fastest.
Arguments:
- tokens: bfloat16 [512, 8192], P('row'), may hold values from -48 to 48
- weight: bfloat16 [8192, 14336], P('col', 'row'), may hold values from -0.0625 to 0.0625
- grad_in: bfloat16 [512, 14336], P('col', 'row'), may hold values from -48 to 48
Outputs:
- act_cov: float32 [8192, 8192], P('row', 'col')
- grad_cov: float32 [14336, 14336], P('row', 'col')
All inputs are finite; a program needn't handle non-finite values.
Results may differ from a plain program's by a relative error of at most 0.004.
Values may be sent and summed in bfloat16 or wider, within the bound.
No kernel may reach another device: no remote copies, remote signals or barrier semaphores. Data moves between devices by JAX's collectives and lax.ppermute only.
A program may use at most 64 MiB of HBM per device.

v0:
```python
import jax
import jax.numpy as jnp
from jax import lax
from jax.sharding import PartitionSpec as P


def from_root(value, axis, source):
    kept = jnp.where(lax.axis_index(axis) == source, value, 0).astype(value.dtype)
    return lax.psum(kept, axis)


def silu_slope(pre_act):
    sigmoid_value = jax.nn.sigmoid(pre_act)
    return sigmoid_value * (1.0 + pre_act * (1.0 - sigmoid_value))


def shards(tokens, weight, grad_in):
    row_count = lax.axis_size("row")
    col_count = lax.axis_size("col")
    col_index = lax.axis_index("col")
    tok_local = tokens.shape[0]
    token_count = tok_local * row_count
    feat_cols = tokens.shape[1] // col_count
    row_ratio = row_count // col_count
    contract = (((0,), (0,)), ((), ()))
    own_blocks = lax.all_to_all(tokens, "row", split_axis=1, concat_axis=0, tiled=True)
    own_cols = lax.dynamic_slice_in_dim(tokens, col_index * feat_cols, feat_cols, 1)
    shard_piece = lax.all_gather(own_cols, "row", axis=0, tiled=True)
    act_running = lax.dot_general(
        own_blocks, shard_piece, contract, preferred_element_type=jnp.float32
    )
    pre_piece = jnp.dot(shard_piece, weight, preferred_element_type=jnp.float32)
    act_cov = act_running / token_count
    pre_act = lax.psum(pre_piece, "col")
    gathered_cot = lax.all_gather(grad_in, "col", axis=0, tiled=True)
    slope_grad = (gathered_cot * silu_slope(pre_act)).astype(jnp.bfloat16)
    tile_parts = []
    for panel_index in range(row_ratio):
        column_panel = from_root(slope_grad, "row", col_index * row_ratio + panel_index)
        tile_parts.append(
            lax.dot_general(slope_grad, column_panel, contract, preferred_element_type=jnp.float32)
        )
    grad_cov = jnp.concatenate(tile_parts, axis=1) / token_count
    return (act_cov, grad_cov)


def solution(mesh):
    placed = (P("row", None), P("col", "row"), P("col", "row"))
    return jax.shard_map(
        shards,
        mesh=mesh,
        in_specs=placed,
        out_specs=(P("row", "col"), P("row", "col")),
        check_vma=False,
    )
```

profile of v0, /device:TPU:8, one launch (start us, length us, event | category | flops | bytes accessed | tf_op | source)
XLA Modules:
  0.0 534.9 jit_solution(4945826662733289264)
XLA Ops:
  7.2 0.0 copy-start
  7.2 0.0 all-reduce.4.cloned.1.call-start
  7.2 0.8 constant_dynamic-slice_fusion
  8.0 0.0 copy-start.2
  8.0 87.6 %all_gather.6 = bf16[512,512]{1,0:T(8,128)(2,1)S(1)} all-gather(bf16[16,512]{1,0:T(8,128)(2,1)S(1)} %constant_dynamic-slice_fusion), channel_id=1, replica_groups=mesh['row'=32,'col'=16] {'row'}, dimensions={0}, use_global_device_ids=true | all-gather | bytes 540672 | tf_op jit(solution)/shard_map/all_gather | solution.py:28
  95.6 0.0 copy-done
  95.6 0.0 copy-start.3
  95.6 1.4 fusion.1
  96.9 0.0 all-reduce.4.cloned.1.call-update
  97.0 0.0 copy-done.2
  97.0 0.7 copy.17
  97.7 3.9 all-to-all-start
  101.6 0.0 all-reduce.6.cloned.1.call-start
  101.6 0.0 copy-done.3
  101.7 18.1 %all_gather.7 = bf16[512,448]{1,0:T(8,128)(2,1)S(1)} all-gather(bf16[32,448]{1,0:T(8,128)(2,1)S(1)} %copy-done.3), channel_id=1, replica_groups=mesh['row'=32,'col'=16] {'col'}, dimensions={0}, use_global_device_ids=true | all-gather | bytes 487424 | tf_op jit(solution)/shard_map/all_gather | solution.py:35
  119.7 0.2 copy.13
  119.9 98.3 %all-reduce.4.cloned.1.call-done = f32[512,448]{0,1:T(8,128)} async-done(((f32[512,448]{0,1:T(8,128)}), f32[512,448]{0,1:T(8,128)}) %all-reduce.4.cloned.1.call-update) | async-done | bytes 917520 | tf_op jit(solution)/shard_map/psum | solution.py:34
  218.2 2.3 broadcast_select_fusion.1
  220.6 0.8 broadcast_select_fusion
  221.4 0.0 all-reduce.6.cloned.1.call-update
  221.4 0.0 all-to-all-done
  221.4 0.3 fusion
  221.8 1.0 copy.14
  222.8 301.9 %all-reduce.6.cloned.1.call-done = (bf16[512,448]{0,1:T(8,128)(2,1)}, bf16[512,448]{0,1:T(8,128)(2,1)}) async-done(((bf16[512,448]{0,1:T(8,128)(2,1)}, bf16[512,448]{0,1:T(8,128)(2,1)}), (bf16[512,448]{0,1:T(8,128)(2,1)}, bf16[512,448]{0,1:T(8,128)(2,1)})) %all-reduce.6.cloned.1.call-update) | async-done | bytes 917520 | tf_op jit(solution)/shard_map/psum | solution.py:9
  524.6 0.0 copy-start.1
  524.6 1.5 fusion.3
  526.1 0.0 copy-done.1
  526.1 0.4 fusion.2
  526.6 1.5 maximum_multiply_fusion
Async XLA Ops:
  7.2 88.4 %copy-start = (bf16[512,448]{0,1:T(8,128)(2,1)S(1)}, bf16[512,448]{0,1:T(8,128)(2,1)}, u32[]{:S(2)}) copy-start(bf16[512,448]{0,1:T(8,128)(2,1)} %param.4) | copy-start | bytes 1376260
  7.2 211.0 %all-reduce.4.cloned.1.call-start = ((), (), s32[]{:S(2)}) async-start(), calls=%async_computation.1 | async-start | bytes 1835008 | tf_op jit(solution)/shard_map/psum | solution.py:34
  8.0 89.0 %copy-start.2 = (bf16[16,8192]{1,0:T(8,128)(2,1)S(1)}, bf16[16,8192]{1,0:T(8,128)(2,1)}, u32[]{:S(2)}) copy-start(bf16[16,8192]{1,0:T(8,128)(2,1)} %param.3) | copy-start | bytes 786436
  95.6 6.1 %copy-start.3 = (bf16[32,448]{1,0:T(8,128)(2,1)S(1)}, bf16[32,448]{1,0:T(8,128)(2,1)}, u32[]{:S(2)}) copy-start(bf16[32,448]{1,0:T(8,128)(2,1)} %param.5) | copy-start | bytes 86020
  97.7 123.7 %all-to-all-start = ((bf16[16,32,256]{2,0,1:T(8,128)(2,1)}), bf16[16,32,256]{2,0,1:T(8,128)(2,1)S(1)}, u32[]{:S(2)}, u32[]{:S(2)}) async-start(bf16[16,32,256]{2,0,1:T(8,128)(2,1)} %bitcast.16), calls=%async_computation | async-start | bytes 524288 | tf_op jit(solution)/shard_map/all_to_all | solution.py:26
  101.6 423.0 %all-reduce.6.cloned.1.call-start = ((), (), s32[]{:S(2)}) async-start(), calls=%async_computation.2 | async-start | bytes 1835008 | tf_op jit(solution)/shard_map/psum | solution.py:9
  524.6 1.5 copy-start.1
Sparse Core Ops, SparseCore 0:
  97.1 121.0 all-reduce.3
  222.1 302.5 all-reduce.5
where the time goes:
time: 535 us
  waiting for transfers between devices  400 us (75%)
  blocking collectives  106 us (20%)
  between operations  14.1 us (3%)
    psum x1, waiting for transfers between devices, from_root(): return lax.psum(kept, axis)  302 us
    psum x1, waiting for transfers between devices, shards(): pre_act = lax.psum(pre_piece, 'col')  98.3 us
    all_gather x1, blocking collectives, shards(): shard_piece = lax.all_gather(own_cols, 'row', axis=0, tiled=True)  87.6 us
    all_gather x1, blocking collectives, shards(): gathered_cot = lax.all_gather(grad_in, 'col', axis=0, tiled=True)  18.1 us
  transfers between devices with their start and end apart: 3, of which 2 were waited for; matrix products, arithmetic and copies ran while one was open for 1% of the time, Pallas kernels for 0%

commit v1 on v0

v1 whole, which is shorter than its diff:
```python
import jax
import jax.numpy as jnp
from jax import lax
from jax.sharding import Mesh, PartitionSpec as P

ROW = ("xh", "z")
COL = ("xl", "y", "core")
LEVEL = ("xh", "xl", "y", "core")
SIZES = (2, 16, 2, 4, 2)
CONTRACT = (((0,), (0,)), ((), ()))
LANES = 512


def exchange(parts, axis):
    return lax.all_to_all(parts, axis, split_axis=0, concat_axis=0, tiled=True)


def silu_slope(pre_act):
    sigmoid_value = jax.nn.sigmoid(pre_act)
    return sigmoid_value * (1.0 + pre_act * (1.0 - sigmoid_value))


def dot(a, b):
    return lax.dot_general(a, b, CONTRACT, preferred_element_type=jnp.float32)


def shards(tokens, weight, grad_in):
    tok, feats = tokens.shape
    hid = weight.shape[1]
    fcol = weight.shape[0]
    nx, nz, _, ny, nc = SIZES
    ncol = 2 * ny * nc
    rfeat = feats // (nx * nz)
    xh, xl, z = (lax.axis_index(a) for a in ("xh", "xl", "z"))
    col = lax.axis_index(COL)
    token_count = tok * nx * nz

    own_cols = lax.dynamic_slice_in_dim(tokens, col * fcol, fcol, 1)
    half = exchange(jnp.broadcast_to(own_cols[None], (nz, tok, fcol)), "z")
    half = half.reshape(nz * tok, fcol)
    swap = [(0, 1), (1, 0)]
    other_weight = lax.ppermute(weight, "xh", swap)
    pair0 = jnp.where(xh == 0, weight, other_weight)
    pair1 = jnp.where(xh == 0, other_weight, weight)

    halves = grad_in.reshape(2, tok, hid)
    squares = [(0, 0), (0, 1), (1, 0), (1, 1)]
    from_a = lax.ppermute(
        jnp.where(xh == 0, halves[0], halves[1]), ("xh", "xl"), [(2 * a + b, 2 * b + a) for a, b in squares]
    )
    from_b = lax.ppermute(
        jnp.where(xh == 0, halves[1], halves[0]), ("xh", "xl"), [(2 * a + b, 2 * b + 1 - a) for a, b in squares]
    )
    cot = jnp.stack([jnp.where(xl == 0, from_a, from_b), jnp.where(xl == 0, from_b, from_a)])

    part = jnp.stack([jnp.dot(half, w, preferred_element_type=jnp.float32) for w in (pair0, pair1)])
    part = part.reshape(nx, ny * nc, 2, tok, hid).transpose(2, 1, 0, 3, 4)
    part = part.reshape(ncol, nx, tok, hid)
    pre_act = jnp.sum(exchange(part, COL), axis=0)
    slope = (cot.astype(jnp.float32) * silu_slope(pre_act)).astype(jnp.bfloat16)
    slope = jnp.pad(slope, ((0, 0), (0, 0), (0, LANES - hid)))

    own_token = lax.dynamic_slice_in_dim(tokens, col, 1, 0).reshape(1, tok, LANES)
    lines = lax.all_gather(jnp.concatenate([slope, own_token], axis=0), "z", axis=0, tiled=False)
    panels = lines[:, :2].reshape(ny * nc, 2, nx, tok, LANES).transpose(2, 0, 1, 3, 4)
    panels = jnp.broadcast_to(panels.reshape(1, ncol, 2 * tok, LANES), (nx, ncol, 2 * tok, LANES))
    rows = jnp.broadcast_to(slope[:, None], (nx, ncol, tok, LANES))
    picked = lines[:, 2].reshape(2, nz // 2, nx, nz // 2, 2, rfeat)
    picked = lax.dynamic_index_in_dim(picked, z // 2, 3, keepdims=False)
    picked = jnp.where(z % 2 == 0, picked[:, :, :, 0], picked[:, :, :, 1])
    picked = picked.transpose(2, 1, 0, 3).reshape(nx, 1, nz // 2, LANES)
    picked = jnp.broadcast_to(picked, (nx, ncol, nz // 2, LANES))
    pieces = jnp.concatenate([rows, panels, picked], axis=2).reshape(nx * ncol, -1, LANES)
    pieces = exchange(pieces, LEVEL)

    row_block = pieces[:, :tok, :hid].reshape(-1, hid)
    tiles = [
        dot(row_block, pieces[:, (1 + b) * tok : (2 + b) * tok, :hid].reshape(-1, hid)) for b in range(2)
    ]
    grad_cov = jnp.concatenate(tiles, axis=1) / token_count

    other_half = lax.ppermute(half, "xh", swap)
    cols = jnp.stack([jnp.where(xh == 0, half, other_half), jnp.where(xh == 0, other_half, half)])
    cols = cols.reshape(nx, 2, nz // 2, tok, fcol).transpose(1, 0, 3, 2, 4).reshape(2, -1, fcol)
    act_rows = pieces[:, 3 * tok :].reshape(-1, LANES)
    act_cov = (dot(act_rows[:, :rfeat], cols[0]) + dot(act_rows[:, rfeat:], cols[1])) / token_count
    return act_cov, grad_cov


def solution(mesh):
    fine = Mesh(mesh.devices.reshape(SIZES), ("xh", "z", "xl", "y", "core"))
    placed = (P(ROW, None), P(COL, ROW), P(COL, ROW))
    return jax.shard_map(
        shards,
        mesh=fine,
        in_specs=placed,
        out_specs=(P(ROW, COL), P(ROW, COL)),
        check_vma=False,
    )
```

time: 535 us -> 138 us (0.26)
  the two profiles are of different devices: /device:TPU:8 before, /device:TPU:1 now
where the time goes in v1:
time: 138 us
  starting transfers between devices  55.5 us (40%)
  waiting for transfers between devices  43.5 us (32%)
  blocking collectives  27.1 us (20%)
  local copies, waits for them, and re-layouts  3.82 us (3%)
  matrix products  3.74 us (3%)
  other arithmetic  3.25 us (2%)
    all_to_all x3, starting transfers between devices, exchange(): return lax.all_to_all(parts, axis, split_axis=0, concat_axis=0, tiled=True)  39 us
    all_gather x1, blocking collectives, shards(): lax.all_gather(jnp.concatenate([slope, own_token], axis=0), 'z', axis=0,...  27.1 us
    ppermute x1, waiting for transfers between devices, shards(): other_half = lax.ppermute(half, 'xh', swap)  24.3 us
    ppermute x1, waiting for transfers between devices, shards(): other_weight = lax.ppermute(weight, 'xh', swap)  10 us
    ppermute x1, waiting for transfers between devices, shards(): lax.ppermute(jnp.where(xh == 0, halves[1], halves[0]), ('xh', 'xl'), [(2...  9.18 us
    ppermute x1, starting transfers between devices, shards(): lax.ppermute(jnp.where(xh == 0, halves[1], halves[0]), ('xh', 'xl'), [(2...  6.32 us
    ppermute x1, starting transfers between devices, shards(): other_half = lax.ppermute(half, 'xh', swap)  4.81 us
    ppermute x1, starting transfers between devices, shards(): other_weight = lax.ppermute(weight, 'xh', swap)  4.65 us
  transfers between devices with their start and end apart: 7, of which 3 were waited for; matrix products, arithmetic and copies ran while one was open for 0% of the time, Pallas kernels for 0%

profile of v1, /device:TPU:1, one launch (start us, length us, event | category | flops | bytes accessed | tf_op | source)
XLA Modules:
  0.0 137.8 jit_solution(8791630072087563457)
XLA Ops:
  0.6 0.0 copy-start
  0.6 0.0 copy-start.1
  0.7 0.9 copy-done
  1.6 0.7 broadcast_in_dim.12
  2.3 15.7 %all-to-all-start = ((bf16[16,16,512]{2,1,0:T(8,128)(2,1)}), bf16[16,16,512]{2,1,0:T(8,128)(2,1)S(1)}, u32[]{:S(2)}, u32[]{:S(2)}) async-start(bf16[16,16,512]{2,1,0:T(8,128)(2,1)} %broadcast_in_dim.12), calls=%async_computation | async-start | bytes 524288 | tf_op jit(solution)/shard_map/all_to_all | solution.py:15
  18.1 4.7 %collective-permute-start.2 = (bf16[512,448]{0,1:T(8,128)(2,1)}, bf16[512,448]{0,1:T(8,128)(2,1)S(1)}, u32[]{:S(2)}, u32[]{:S(2)}) collective-permute-start(bf16[512,448]{0,1:T(8,128)(2,1)} %param.4), channel_id=1, source_target_pairs={{0,256},{256,0},{1,257},{257,1},{2,258},{258,2},{3,259},{259,3},{4... | collective-permute-start | bytes 1376264 | tf_op jit(solution)/shard_map/ppermute | solution.py:42
  22.7 10.0 %collective-permute-done.2 = bf16[512,448]{0,1:T(8,128)(2,1)S(1)} collective-permute-done((bf16[512,448]{0,1:T(8,128)(2,1)}, bf16[512,448]{0,1:T(8,128)(2,1)S(1)}, u32[]{:S(2)}, u32[]{:S(2)}) %collective-permute-start.2) | collective-permute-done | bytes 458784 | tf_op jit(solution)/shard_map/ppermute | solution.py:42
  32.8 0.0 all-to-all-done
  32.8 0.3 convolution_bitcast_fusion.2
  33.1 0.0 copy-done.1
  33.1 0.3 convolution_bitcast_fusion.3
  33.4 0.1 maximum_bitcast_fusion
  33.6 0.0 copy-start.2
  33.6 1.1 copy.30
  34.7 10.0 %all-to-all-start.1 = ((f32[16,2,16,448]{3,2,1,0:T(8,128)}), f32[16,2,16,448]{3,2,1,0:T(8,128)S(1)}, u32[]{:S(2)}, u32[]{:S(2)}) async-start(f32[16,2,16,448]{3,2,1,0:T(8,128)} %bitcast.10), calls=%async_computation.1 | async-start | bytes 2097152 | tf_op jit(solution)/shard_map/all_to_all | solution.py:15
  44.7 0.0 copy-done.2
  44.7 0.7 collective-permute-start
  45.4 6.3 %collective-permute-start.1 = (bf16[16,448]{1,0:T(8,128)(2,1)S(1)}, bf16[16,448]{1,0:T(8,128)(2,1)S(1)}, u32[]{:S(2)}, u32[]{:S(2)}) collective-permute-start(bf16[16,448]{1,0:T(8,128)(2,1)S(1)} %get-tuple-element.12), channel_id=1, source_target_pairs={{0,8},{8,264},{256,0},{264,256},{1,9},{9,265},{257,1},{265,257},{2... | collective-permute-start | bytes 43016 | tf_op jit(solution)/shard_map/ppermute | solution.py:51
  51.7 0.1 dynamic-slice_reduce_fusion
  51.9 0.0 collective-permute-done
  51.9 9.2 %collective-permute-done.1 = bf16[16,448]{1,0:T(8,128)(2,1)S(1)} collective-permute-done((bf16[16,448]{1,0:T(8,128)(2,1)S(1)}, bf16[16,448]{1,0:T(8,128)(2,1)S(1)}, u32[]{:S(2)}, u32[]{:S(2)}) %collective-permute-start.1) | collective-permute-done | bytes 14368 | tf_op jit(solution)/shard_map/ppermute | solution.py:51
  61.1 0.0 all-to-all-done.1
  61.1 0.1 reduce_sum.9
  61.3 27.1 %all-gather = bf16[48,16,512]{2,1,0:T(8,128)(2,1)S(1)} all-gather(bf16[3,16,512]{2,1,0:T(8,128)(2,1)S(1)} %pad_maximum_fusion.1), channel_id=2, replica_groups=mesh['xh'=2,'z'=16,'xl'=2,'y'=4,'core'=2] {'z'}, dimensions={0}, use_global_device_ids=true | all-gather | bytes 835584 | tf_op jit(solution)/shard_map/all_gather | solution.py:64
  88.4 0.1 reshape_squeeze.3
  88.6 0.1 broadcast_in_dim.13
  88.7 0.1 broadcast_in_dim.29
  88.8 1.4 %pad_maximum_fusion = bf16[2,16,56,512]{3,2,1,0:T(8,128)(2,1)} fusion(bf16[2,16,8,512]{3,2,1,0:T(8,128)(2,1)S(1)} %broadcast_in_dim.31, bf16[2,16,32,512]{3,2,1,0:T(8,128)(2,1)S(1)} %broadcast_in_dim.29, bf16[2,16,16,512]{3,2,1,0:T(8,128)(2,1)S(1)} %broadcast_in_dim.13), kind=kLoop, calls=%fused_computation | loop fusion | flops 5505024 | bytes 3670016 | tf_op jit(solution)/shard_map/concatenate | solution.py:73
  90.2 13.2 %all-to-all-start.2 = ((bf16[32,56,512]{2,1,0:T(8,128)(2,1)}), bf16[32,56,512]{2,1,0:T(8,128)(2,1)S(1)}, u32[]{:S(2)}, u32[]{:S(2)}) async-start(bf16[32,56,512]{2,1,0:T(8,128)(2,1)} %bitcast.63), calls=%async_computation.2 | async-start | bytes 3670016 | tf_op jit(solution)/shard_map/all_to_all | solution.py:15
  103.5 4.8 %collective-permute-start.3 = (bf16[256,512]{1,0:T(8,128)(2,1)S(1)}, bf16[256,512]{1,0:T(8,128)(2,1)S(1)}, u32[]{:S(2)}, u32[]{:S(2)}) collective-permute-start(bf16[256,512]{1,0:T(8,128)(2,1)S(1)} %bitcast.66), channel_id=1, source_target_pairs={{0,256},{256,0},{1,257},{257,1},{2,258},{258,2},{3,259},{259,3},{4... | collective-permute-start | bytes 786440 | tf_op jit(solution)/shard_map/ppermute | solution.py:82
  108.3 24.3 %collective-permute-done.3 = bf16[256,512]{1,0:T(8,128)(2,1)S(1)} collective-permute-done((bf16[256,512]{1,0:T(8,128)(2,1)S(1)}, bf16[256,512]{1,0:T(8,128)(2,1)S(1)}, u32[]{:S(2)}, u32[]{:S(2)}) %collective-permute-start.3) | collective-permute-done | bytes 262176 | tf_op jit(solution)/shard_map/ppermute | solution.py:82
  132.6 0.1 broadcast_select_fusion.1
  132.6 0.1 maximum_bitcast_fusion.1
  132.7 0.2 copy.36
  132.9 0.2 copy.35
  133.0 0.0 all-to-all-done.2
  133.1 0.2 fusion.15
  133.2 0.9 convolution_bitcast_fusion.1
  134.1 0.9 convolution_bitcast_fusion
  135.0 0.2 fusion.12
  135.3 1.1 fusion
  136.4 1.5 %maximum_multiply_fusion = f32[448,896]{1,0:T(8,128)} fusion(f32[448,448]{1,0:T(8,128)S(1)} %convolution_bitcast_fusion, f32[448,448]{1,0:T(8,128)S(1)} %convolution_bitcast_fusion.1), kind=kLoop, calls=%fused_computation.1 | loop fusion | flops 802816 | bytes 3211264 | tf_op jit(solution)/shard_map/div | solution.py:80
  (17 shorter events, 0.3 us)
Async XLA Ops:
  0.6 1.0 copy-start
  0.6 32.5 %copy-start.1 = (bf16[512,448]{0,1:T(8,128)(2,1)S(1)}, bf16[512,448]{0,1:T(8,128)(2,1)}, u32[]{:S(2)}) copy-start(bf16[512,448]{0,1:T(8,128)(2,1)} %param.4) | copy-start | bytes 1376260
  2.3 30.4 %all-to-all-start = ((bf16[16,16,512]{2,1,0:T(8,128)(2,1)}), bf16[16,16,512]{2,1,0:T(8,128)(2,1)S(1)}, u32[]{:S(2)}, u32[]{:S(2)}) async-start(bf16[16,16,512]{2,1,0:T(8,128)(2,1)} %broadcast_in_dim.12), calls=%async_computation | async-start | bytes 524288 | tf_op jit(solution)/shard_map/all_to_all | solution.py:15
  18.1 14.7 %collective-permute-start.2 = (bf16[512,448]{0,1:T(8,128)(2,1)}, bf16[512,448]{0,1:T(8,128)(2,1)S(1)}, u32[]{:S(2)}, u32[]{:S(2)}) collective-permute-start(bf16[512,448]{0,1:T(8,128)(2,1)} %param.4), channel_id=1, source_target_pairs={{0,256},{256,0},{1,257},{257,1},{2,258},{258,2},{3,259},{259,3},{4... | collective-permute-start | bytes 1376264 | tf_op jit(solution)/shard_map/ppermute | solution.py:42
  33.6 11.1 %copy-start.2 = (bf16[32,448]{1,0:T(8,128)(2,1)S(1)}, bf16[32,448]{1,0:T(8,128)(2,1)}, u32[]{:S(2)}) copy-start(bf16[32,448]{1,0:T(8,128)(2,1)} %param.5) | copy-start | bytes 86020
  34.7 26.4 %all-to-all-start.1 = ((f32[16,2,16,448]{3,2,1,0:T(8,128)}), f32[16,2,16,448]{3,2,1,0:T(8,128)S(1)}, u32[]{:S(2)}, u32[]{:S(2)}) async-start(f32[16,2,16,448]{3,2,1,0:T(8,128)} %bitcast.10), calls=%async_computation.1 | async-start | bytes 2097152 | tf_op jit(solution)/shard_map/all_to_all | solution.py:15
  44.7 7.2 %collective-permute-start = (bf16[16,448]{1,0:T(8,128)(2,1)S(1)}, bf16[16,448]{1,0:T(8,128)(2,1)S(1)}, u32[]{:S(2)}, u32[]{:S(2)}) collective-permute-start(bf16[16,448]{1,0:T(8,128)(2,1)S(1)} %get-tuple-element.11), channel_id=1, source_target_pairs={{0,0},{8,256},{256,8},{264,264},{1,1},{9,257},{257,9},{265,265},{2... | collective-permute-start | bytes 43016 | tf_op jit(solution)/shard_map/ppermute | solution.py:48
  45.4 15.7 %collective-permute-start.1 = (bf16[16,448]{1,0:T(8,128)(2,1)S(1)}, bf16[16,448]{1,0:T(8,128)(2,1)S(1)}, u32[]{:S(2)}, u32[]{:S(2)}) collective-permute-start(bf16[16,448]{1,0:T(8,128)(2,1)S(1)} %get-tuple-element.12), channel_id=1, source_target_pairs={{0,8},{8,264},{256,0},{264,256},{1,9},{9,265},{257,1},{265,257},{2... | collective-permute-start | bytes 43016 | tf_op jit(solution)/shard_map/ppermute | solution.py:51
  90.2 42.8 %all-to-all-start.2 = ((bf16[32,56,512]{2,1,0:T(8,128)(2,1)}), bf16[32,56,512]{2,1,0:T(8,128)(2,1)S(1)}, u32[]{:S(2)}, u32[]{:S(2)}) async-start(bf16[32,56,512]{2,1,0:T(8,128)(2,1)} %bitcast.63), calls=%async_computation.2 | async-start | bytes 3670016 | tf_op jit(solution)/shard_map/all_to_all | solution.py:15
  103.5 29.1 %collective-permute-start.3 = (bf16[256,512]{1,0:T(8,128)(2,1)S(1)}, bf16[256,512]{1,0:T(8,128)(2,1)S(1)}, u32[]{:S(2)}, u32[]{:S(2)}) collective-permute-start(bf16[256,512]{1,0:T(8,128)(2,1)S(1)} %bitcast.66), channel_id=1, source_target_pairs={{0,256},{256,0},{1,257},{257,1},{2,258},{258,2},{3,259},{259,3},{4... | collective-permute-start | bytes 786440 | tf_op jit(solution)/shard_map/ppermute | solution.py:82

commit v2 on v1

v2 whole, which is shorter than its diff:
```python
import jax
import jax.numpy as jnp
from jax import lax
from jax.sharding import Mesh, PartitionSpec as P

ROW = ("xh", "z")
COL = ("xl", "y", "core")
LEVEL = ("xh", "xl", "y", "core")
SIZES = (2, 16, 2, 4, 2)
CONTRACT = (((0,), (0,)), ((), ()))
LANES = 512


def exchange(parts, axis):
    return lax.all_to_all(parts, axis, split_axis=0, concat_axis=0, tiled=True)


def silu_slope(pre_act):
    sigmoid_value = jax.nn.sigmoid(pre_act)
    return sigmoid_value * (1.0 + pre_act * (1.0 - sigmoid_value))


def dot(a, b):
    return lax.dot_general(a, b, CONTRACT, preferred_element_type=jnp.float32)


def to_tiles(x):
    lead, (rows, lanes) = x.shape[:-2], x.shape[-2:]
    x = x.reshape(*lead, rows // 8, 8, lanes // 128, 128)
    return jnp.swapaxes(x, -3, -2).reshape(*lead, -1, 8, 128)


def from_tiles(x, rows):
    lead = x.shape[:-3]
    x = x.reshape(*lead, rows // 8, -1, 8, 128)
    return jnp.swapaxes(x, -3, -2).reshape(*lead, rows, -1)


def moves(source_bit):
    pairs = []
    for xh in range(2):
        for xl in range(2):
            for k in range(8):
                source = (xh * 2 + xl) * 8 + k
                core = xh if source_bit == 0 else 1 - xh
                pairs.append((source, ((xl * 2 + k // 4) * 4 + k % 4) * 2 + core))
    return pairs


def shards(tokens, weight, grad_in):
    tok, feats = tokens.shape
    hid = weight.shape[1]
    fcol = weight.shape[0]
    nx, nz, _, ny, nc = SIZES
    ncol = 2 * ny * nc
    rfeat = feats // (nx * nz)
    xh, z, core = (lax.axis_index(a) for a in ("xh", "z", "core"))
    col = lax.axis_index(COL)
    token_count = tok * nx * nz

    own_cols = lax.dynamic_slice_in_dim(tokens, col * fcol, fcol, 1)
    half = exchange(jnp.broadcast_to(own_cols[None], (nz, tok, fcol)), "z")
    half = half.reshape(nz * tok, fcol)
    swap = [(0, 1), (1, 0)]
    own_weight = weight.T
    received = lax.ppermute(jnp.concatenate([own_weight, own_cols], axis=0), "xh", swap)
    other_weight, other_cols = received[:hid], received[hid:]

    halves = grad_in.reshape(2, tok, hid)
    from_a = lax.ppermute(jnp.where(xh == 0, halves[0], halves[1]), LEVEL, moves(0))
    from_b = lax.ppermute(jnp.where(xh == 0, halves[1], halves[0]), LEVEL, moves(1))
    own_first = core == xh
    cot = jnp.concatenate(
        [jnp.where(own_first, from_a, from_b), jnp.where(own_first, from_b, from_a)], axis=1
    )
    half, cot = lax.optimization_barrier((half, cot))

    both = jnp.concatenate([own_weight, other_weight], axis=0)
    part = lax.dot_general(half, both, (((1,), (1,)), ((), ())), preferred_element_type=jnp.float32)
    part = part.astype(jnp.bfloat16).reshape(ncol, tok, 2 * hid)
    pre_act = jnp.sum(exchange(part, COL).astype(jnp.float32), axis=0)
    slope = (cot.astype(jnp.float32) * silu_slope(pre_act)).astype(jnp.bfloat16)
    own, other = slope[:, :hid], slope[:, hid:]
    slope = jnp.stack([jnp.where(xh == 0, own, other), jnp.where(xh == 0, other, own)])
    wide = jnp.pad(slope, ((0, 0), (0, 0), (0, LANES - hid)))
    wide = to_tiles(wide)
    n_row = wide.shape[1]

    own_token = lax.dynamic_slice_in_dim(tokens, col, 1, 0).reshape(-1, 8, 128)
    pair = to_tiles(jnp.concatenate([slope[0], slope[1]], axis=1))
    sent = jnp.concatenate([pair, own_token, to_tiles(other_cols)], axis=0)
    n_slope, n_token = pair.shape[0], own_token.shape[0]
    lines = lax.all_gather(sent, "z", axis=0, tiled=False)
    blocks = from_tiles(lines[:, :n_slope], tok).reshape(nz // 2, 2, tok, 2 * hid)
    panels = jnp.stack(
        [
            jnp.concatenate([blocks[:, 0, :, :hid], blocks[:, 1, :, :hid]], axis=-1),
            jnp.concatenate([blocks[:, 0, :, hid:], blocks[:, 1, :, hid:]], axis=-1),
        ]
    )
    panels = to_tiles(panels.reshape(ncol, tok, 2 * hid))
    n_panel = panels.shape[1]
    panels = jnp.broadcast_to(panels[None], (nx, *panels.shape))

    rows = jnp.broadcast_to(wide[:, None], (nx, ncol, n_row, 8, 128))
    picked = lines[:, n_slope : n_slope + n_token].reshape(2, nz // 2, nx, nz, 2, 128)
    picked = lax.dynamic_index_in_dim(picked, z, 3, keepdims=False)
    picked = picked.transpose(2, 0, 3, 1, 4).reshape(nx, 1, 4, nz // 2, 128)
    picked = jnp.broadcast_to(picked, (nx, ncol, 4, nz // 2, 128))
    pieces = jnp.concatenate([panels, rows, picked], axis=2).reshape(nx * ncol, -1, 8, 128)
    pieces = exchange(pieces, LEVEL)

    panel = from_tiles(pieces[:, :n_panel], tok).reshape(-1, 2 * hid)
    row_block = from_tiles(pieces[:, n_panel : n_panel + n_row], tok).reshape(-1, LANES)[:, :hid]
    grad_cov = dot(row_block, panel) / token_count

    other_half = from_tiles(lines[:, n_slope + n_token :], tok).reshape(nz * tok, fcol)
    cols = jnp.stack([jnp.where(xh == 0, half, other_half), jnp.where(xh == 0, other_half, half)])
    cols = cols.reshape(nx, nz, tok, fcol).transpose(0, 2, 1, 3).reshape(-1, fcol)
    act_rows = pieces[:, n_panel + n_row :].reshape(nx * ncol, 2, 2, nz // 2, 128)
    act_rows = act_rows.transpose(0, 1, 3, 2, 4).reshape(-1, rfeat)
    act_cov = dot(act_rows, cols) / token_count
    return act_cov, grad_cov


def solution(mesh):
    fine = Mesh(mesh.devices.reshape(SIZES), ("xh", "z", "xl", "y", "core"))
    placed = (P(ROW, None), P(COL, ROW), P(COL, ROW))
    return jax.shard_map(
        shards,
        mesh=fine,
        in_specs=placed,
        out_specs=(P(ROW, COL), P(ROW, COL)),
        check_vma=False,
    )
```

time: 138 us -> 124 us (0.90)
  starting transfers between devices: 55.5 us -> 47.7 us
  waiting for transfers between devices: 43.5 us -> 36.5 us
  blocking collectives: 27.1 us -> 28.6 us
    ppermute x4 -> x3, waiting for transfers between devices: 43.5 us -> 3.82 us  [the longest x1 3.82 us: shards(): lax.ppermute(jnp.where(xh == 0, halves[0], halves[1]), LEVEL, moves(0))]
    all_to_all x3, waiting for transfers between devices: 0.01 us -> 32.6 us  [exchange(): return lax.all_to_all(parts, axis, split_axis=0, concat_axis=0, tiled=True)]
    all_to_all x3, starting transfers between devices: 39 us -> 34.8 us  [exchange(): return lax.all_to_all(parts, axis, split_axis=0, concat_axis=0, tiled=True)]
    ppermute x4 -> x3, starting transfers between devices: 16.4 us -> 12.9 us  [the longest x1 4.65 us: shards(): lax.ppermute(jnp.concatenate([own_weight, own_cols], axis=0), 'xh', swap)]
    all_gather x1, blocking collectives: 27.1 us -> 28.6 us  [shards(): lines = lax.all_gather(sent, 'z', axis=0, tiled=False)]
    div x1 -> x0, other arithmetic: 1.46 us -> none  [shards(): grad_cov = jnp.concatenate(tiles, axis=1) / token_count]
    dot_general x4 -> x2, matrix products: 3.07 us -> 2.94 us  [dot(): return lax.dot_general(a, b, CONTRACT, preferred_element_type=jnp.float32)]
  transfers between devices with their start and end apart: 7 -> 6, of which waited for: 3 -> 3; matrix products, arithmetic and copies ran while one was open for 0% -> 1% of each run, Pallas kernels for 0% -> 0%
where the time goes in v2:
time: 124 us
  starting transfers between devices  47.7 us (38%)
  waiting for transfers between devices  36.5 us (29%)
  blocking collectives  28.6 us (23%)
  matrix products  4.18 us (3%)
  other arithmetic  3.13 us (3%)
  local copies, waits for them, and re-layouts  2.9 us (2%)
    all_to_all x3, starting transfers between devices, exchange(): return lax.all_to_all(parts, axis, split_axis=0, concat_axis=0, tiled=True)  34.8 us
    all_to_all x3, waiting for transfers between devices, exchange(): return lax.all_to_all(parts, axis, split_axis=0, concat_axis=0, tiled=True)  32.6 us
    all_gather x1, blocking collectives, shards(): lines = lax.all_gather(sent, 'z', axis=0, tiled=False)  28.6 us
    ppermute x1, starting transfers between devices, shards(): lax.ppermute(jnp.concatenate([own_weight, own_cols], axis=0), 'xh', swap)  4.65 us
    ppermute x1, starting transfers between devices, shards(): lax.ppermute(jnp.where(xh == 0, halves[0], halves[1]), LEVEL, moves(0))  4.33 us
    ppermute x1, starting transfers between devices, shards(): lax.ppermute(jnp.where(xh == 0, halves[1], halves[0]), LEVEL, moves(1))  3.92 us
    ppermute x1, waiting for transfers between devices, shards(): lax.ppermute(jnp.where(xh == 0, halves[0], halves[1]), LEVEL, moves(0))  3.82 us
    dot_general x2, matrix products, dot(): return lax.dot_general(a, b, CONTRACT, preferred_element_type=jnp.float32)  2.94 us
  transfers between devices with their start and end apart: 6, of which 3 were waited for; matrix products, arithmetic and copies ran while one was open for 1% of the time, Pallas kernels for 0%

profile of v2, /device:TPU:1, one launch (start us, length us, event | category | flops | bytes accessed | tf_op | source)
XLA Modules:
  0.0 123.9 jit_solution(17464446410810143307)
XLA Ops:
  0.6 0.0 copy-start
  0.6 0.0 copy-start.1
  0.7 0.0 copy-start.2
  0.7 0.9 copy-done
  1.6 0.7 broadcast_in_dim.27
  2.3 15.7 %all-to-all-start = ((bf16[16,16,512]{2,1,0:T(8,128)(2,1)}), bf16[16,16,512]{2,1,0:T(8,128)(2,1)S(1)}, u32[]{:S(2)}, u32[]{:S(2)}) async-start(bf16[16,16,512]{2,1,0:T(8,128)(2,1)} %broadcast_in_dim.27), calls=%async_computation | async-start | bytes 524288 | tf_op jit(solution)/shard_map/all_to_all | solution.py:15
  18.1 1.1 pad_maximum_fusion.1
  19.1 4.7 %collective-permute-start.2 = (bf16[464,512]{1,0:T(8,128)(2,1)S(1)}, bf16[464,512]{1,0:T(8,128)(2,1)S(1)}, u32[]{:S(2)}, u32[]{:S(2)}) collective-permute-start(bf16[464,512]{1,0:T(8,128)(2,1)S(1)} %pad_maximum_fusion.1), channel_id=1, source_target_pairs={{0,256},{256,0},{1,257},{257,1},{2,258},{258,2},{3,259},{259,3},{4... | collective-permute-start | bytes 1425416 | tf_op jit(solution)/shard_map/ppermute | solution.py:66
  23.8 0.0 copy-done.2
  23.8 4.3 %collective-permute-start = (bf16[16,448]{1,0:T(8,128)(2,1)S(1)}, bf16[16,448]{1,0:T(8,128)(2,1)S(1)}, u32[]{:S(2)}, u32[]{:S(2)}) collective-permute-start(bf16[16,448]{1,0:T(8,128)(2,1)S(1)} %get-tuple-element.16), channel_id=1, source_target_pairs={{0,0},{1,2},{2,4},{3,6},{4,8},{5,10},{6,12},{7,14},{8,256},{9,258}... | collective-permute-start | bytes 43016 | tf_op jit(solution)/shard_map/ppermute | solution.py:70
  28.2 3.9 %collective-permute-start.1 = (bf16[16,448]{1,0:T(8,128)(2,1)S(1)}, bf16[16,448]{1,0:T(8,128)(2,1)S(1)}, u32[]{:S(2)}, u32[]{:S(2)}) collective-permute-start(bf16[16,448]{1,0:T(8,128)(2,1)S(1)} %get-tuple-element.17), channel_id=1, source_target_pairs={{0,1},{1,3},{2,5},{3,7},{4,9},{5,11},{6,13},{7,15},{8,257},{9,259}... | collective-permute-start | bytes 43016 | tf_op jit(solution)/shard_map/ppermute | solution.py:71
  32.1 3.8 %collective-permute-done = bf16[16,448]{1,0:T(8,128)(2,1)S(1)} collective-permute-done((bf16[16,448]{1,0:T(8,128)(2,1)S(1)}, bf16[16,448]{1,0:T(8,128)(2,1)S(1)}, u32[]{:S(2)}, u32[]{:S(2)}) %collective-permute-start) | collective-permute-done | bytes 14368 | tf_op jit(solution)/shard_map/ppermute | solution.py:70
  35.9 0.0 collective-permute-done.1
  35.9 0.1 pad_maximum_fusion.4
  36.0 0.0 collective-permute-done.2
  36.0 0.0 all-to-all-done
  36.1 0.0 copy-done.1
  36.1 1.2 convolution_convert_fusion
  37.3 6.9 %all-to-all-start.1 = ((bf16[16,16,896]{2,1,0:T(8,128)(2,1)}), bf16[16,16,896]{2,1,0:T(8,128)(2,1)S(1)}, u32[]{:S(2)}, u32[]{:S(2)}) async-start(bf16[16,16,896]{2,1,0:T(8,128)(2,1)} %bitcast.2), calls=%async_computation.1 | async-start | bytes 917504 | tf_op jit(solution)/shard_map/all_to_all | solution.py:15
  44.2 0.1 dynamic-slice_reduce_fusion
  44.3 9.0 %all-to-all-done.1 = bf16[16,16,896]{2,1,0:T(8,128)(2,1)S(1)} async-done(((bf16[16,16,896]{2,1,0:T(8,128)(2,1)}), bf16[16,16,896]{2,1,0:T(8,128)(2,1)S(1)}, u32[]{:S(2)}, u32[]{:S(2)}) %all-to-all-start.1) | async-done | bytes 458784 | tf_op jit(solution)/shard_map/all_to_all | solution.py:15
  53.3 0.1 convert_reduce_fusion
  53.4 0.1 broadcast_select_fusion.5
  53.5 0.1 pad_maximum_fusion.5
  53.6 28.6 %all-gather = bf16[480,8,128]{2,1,0:T(8,128)(2,1)S(1)} all-gather(bf16[30,8,128]{2,1,0:T(8,128)(2,1)S(1)} %pad_maximum_fusion.3), channel_id=2, replica_groups=mesh['xh'=2,'z'=16,'xl'=2,'y'=4,'core'=2] {'z'}, dimensions={0}, use_global_device_ids=true | all-gather | bytes 1044480 | tf_op jit(solution)/shard_map/all_gather | solution.py:93
  82.2 0.1 slice_bitcast_fusion.3
  82.4 0.2 copy.26
  82.6 0.2 maximum_bitcast_fusion.1
  82.8 0.1 pad_maximum_fusion.2
  82.8 0.1 broadcast_in_dim.31
  83.0 0.1 broadcast_in_dim.29
  83.1 1.4 %pad_maximum_fusion = bf16[2,16,26,8,128]{4,3,2,1,0:T(8,128)(2,1)} fusion(bf16[2,16,4,8,128]{4,3,2,1,0:T(8,128)(2,1)S(1)} %broadcast_in_dim.33, bf16[2,16,8,8,128]{4,3,2,1,0:T(8,128)(2,1)S(1)} %broadcast_in_dim.31, bf16[2,16,14,8,128]{4,3,2,1,0:T(8,128)(2,1)S(1)} %broadcast_in_dim.29), kind=kLoop, calls=%fused_computation | loop fusion | flops 1703936 | bytes 3407872 | tf_op jit(solution)/shard_map/concatenate | solution.py:110
  84.5 12.2 %all-to-all-start.2 = ((bf16[32,26,8,128]{3,2,1,0:T(8,128)(2,1)}), bf16[32,26,8,128]{3,2,1,0:T(8,128)(2,1)S(1)}, u32[]{:S(2)}, u32[]{:S(2)}) async-start(bf16[32,26,8,128]{3,2,1,0:T(8,128)(2,1)} %bitcast.86), calls=%async_computation.2 | async-start | bytes 3407872 | tf_op jit(solution)/shard_map/all_to_all | solution.py:15
  96.8 0.1 maximum_bitcast_fusion
  96.8 0.3 copy.29
  97.1 23.7 %all-to-all-done.2 = bf16[32,26,8,128]{3,2,1,0:T(8,128)(2,1)S(1)} async-done(((bf16[32,26,8,128]{3,2,1,0:T(8,128)(2,1)}), bf16[32,26,8,128]{3,2,1,0:T(8,128)(2,1)S(1)}, u32[]{:S(2)}, u32[]{:S(2)}) %all-to-all-start.2) | async-done | bytes 1703968 | tf_op jit(solution)/shard_map/all_to_all | solution.py:15
  120.8 1.1 convolution_multiply_fusion.1
  121.9 0.1 slice.84
  122.0 0.1 slice.86
  122.1 1.8 %convolution_multiply_fusion = f32[448,896]{1,0:T(8,128)} fusion(bf16[512,896]{1,0:T(8,128)(2,1)S(1)} %bitcast.89, bf16[512,512]{1,0:T(8,128)(2,1)S(1)} %bitcast.92), kind=kOutput, calls=%fused_computation.1 | convolution fusion | flops 411443200 | bytes 3047424 | tf_op jit(solution)/shard_map/dot_general | solution.py:24
  (15 shorter events, 0.3 us)
Async XLA Ops:
  0.6 1.0 copy-start
  0.6 35.4 %copy-start.1 = (bf16[512,448]{0,1:T(8,128)(2,1)S(1)}, bf16[512,448]{0,1:T(8,128)(2,1)}, u32[]{:S(2)}) copy-start(bf16[512,448]{0,1:T(8,128)(2,1)} %param.4) | copy-start | bytes 1376260
  0.7 23.1 %copy-start.2 = (bf16[32,448]{1,0:T(8,128)(2,1)S(1)}, bf16[32,448]{1,0:T(8,128)(2,1)}, u32[]{:S(2)}) copy-start(bf16[32,448]{1,0:T(8,128)(2,1)} %param.5) | copy-start | bytes 86020
  2.3 33.7 %all-to-all-start = ((bf16[16,16,512]{2,1,0:T(8,128)(2,1)}), bf16[16,16,512]{2,1,0:T(8,128)(2,1)S(1)}, u32[]{:S(2)}, u32[]{:S(2)}) async-start(bf16[16,16,512]{2,1,0:T(8,128)(2,1)} %broadcast_in_dim.27), calls=%async_computation | async-start | bytes 524288 | tf_op jit(solution)/shard_map/all_to_all | solution.py:15
  19.1 16.9 %collective-permute-start.2 = (bf16[464,512]{1,0:T(8,128)(2,1)S(1)}, bf16[464,512]{1,0:T(8,128)(2,1)S(1)}, u32[]{:S(2)}, u32[]{:S(2)}) collective-permute-start(bf16[464,512]{1,0:T(8,128)(2,1)S(1)} %pad_maximum_fusion.1), channel_id=1, source_target_pairs={{0,256},{256,0},{1,257},{257,1},{2,258},{258,2},{3,259},{259,3},{4... | collective-permute-start | bytes 1425416 | tf_op jit(solution)/shard_map/ppermute | solution.py:66
  23.8 12.1 %collective-permute-start = (bf16[16,448]{1,0:T(8,128)(2,1)S(1)}, bf16[16,448]{1,0:T(8,128)(2,1)S(1)}, u32[]{:S(2)}, u32[]{:S(2)}) collective-permute-start(bf16[16,448]{1,0:T(8,128)(2,1)S(1)} %get-tuple-element.16), channel_id=1, source_target_pairs={{0,0},{1,2},{2,4},{3,6},{4,8},{5,10},{6,12},{7,14},{8,256},{9,258}... | collective-permute-start | bytes 43016 | tf_op jit(solution)/shard_map/ppermute | solution.py:70
  28.2 7.8 %collective-permute-start.1 = (bf16[16,448]{1,0:T(8,128)(2,1)S(1)}, bf16[16,448]{1,0:T(8,128)(2,1)S(1)}, u32[]{:S(2)}, u32[]{:S(2)}) collective-permute-start(bf16[16,448]{1,0:T(8,128)(2,1)S(1)} %get-tuple-element.17), channel_id=1, source_target_pairs={{0,1},{1,3},{2,5},{3,7},{4,9},{5,11},{6,13},{7,15},{8,257},{9,259}... | collective-permute-start | bytes 43016 | tf_op jit(solution)/shard_map/ppermute | solution.py:71
  37.3 16.0 %all-to-all-start.1 = ((bf16[16,16,896]{2,1,0:T(8,128)(2,1)}), bf16[16,16,896]{2,1,0:T(8,128)(2,1)S(1)}, u32[]{:S(2)}, u32[]{:S(2)}) async-start(bf16[16,16,896]{2,1,0:T(8,128)(2,1)} %bitcast.2), calls=%async_computation.1 | async-start | bytes 917504 | tf_op jit(solution)/shard_map/all_to_all | solution.py:15
  84.5 36.3 %all-to-all-start.2 = ((bf16[32,26,8,128]{3,2,1,0:T(8,128)(2,1)}), bf16[32,26,8,128]{3,2,1,0:T(8,128)(2,1)S(1)}, u32[]{:S(2)}, u32[]{:S(2)}) async-start(bf16[32,26,8,128]{3,2,1,0:T(8,128)(2,1)} %bitcast.86), calls=%async_computation.2 | async-start | bytes 3407872 | tf_op jit(solution)/shard_map/all_to_all | solution.py:15

commit v3 on v2

v3 whole, which is shorter than its diff:
```python
import jax
import jax.numpy as jnp
from jax import lax
from jax.sharding import Mesh, PartitionSpec as P

AXES = ("xh", "zq", "zp", "xl", "y", "core")
SIZES = (2, 8, 2, 2, 4, 2)
ROW = ("xh", "zq", "zp")
LINE = ("zq", "zp")
COL = ("xl", "y", "core")
LEVEL = ("xh", "xl", "y", "core")
LEVELS = ("xh", "zp", "xl", "y", "core")
CONTRACT = (((0,), (0,)), ((), ()))
LANES = 512


def exchange(parts, axis):
    return lax.all_to_all(parts, axis, split_axis=0, concat_axis=0, tiled=True)


def silu_slope(pre_act):
    sigmoid_value = jax.nn.sigmoid(pre_act)
    return sigmoid_value * (1.0 + pre_act * (1.0 - sigmoid_value))


def dot(a, b):
    return lax.dot_general(a, b, CONTRACT, preferred_element_type=jnp.float32)


def to_tiles(x):
    lead, (rows, lanes) = x.shape[:-2], x.shape[-2:]
    x = x.reshape(*lead, rows // 8, 8, lanes // 128, 128)
    return jnp.swapaxes(x, -3, -2).reshape(*lead, -1, 8, 128)


def from_tiles(x, rows):
    lead = x.shape[:-3]
    x = x.reshape(*lead, rows // 8, -1, 8, 128)
    return jnp.swapaxes(x, -3, -2).reshape(*lead, rows, -1)


def moves(source_bit):
    pairs = []
    for xh in range(2):
        for xl in range(2):
            for k in range(8):
                source = (xh * 2 + xl) * 8 + k
                core = xh if source_bit == 0 else 1 - xh
                pairs.append((source, ((xl * 2 + k // 4) * 4 + k % 4) * 2 + core))
    return pairs


def shards(tokens, weight, grad_in):
    tok, feats = tokens.shape
    hid = weight.shape[1]
    fcol = weight.shape[0]
    nx, nq, npar, _, ny, nc = SIZES
    nz = nq * npar
    ncol = 2 * ny * nc
    rfeat = feats // (nx * nz)
    xh, core = lax.axis_index("xh"), lax.axis_index("core")
    col = lax.axis_index(COL)
    token_count = tok * nx * nz

    own_cols = lax.dynamic_slice_in_dim(tokens, col * fcol, fcol, 1)
    own_token = lax.dynamic_slice_in_dim(tokens, col, 1, 0).reshape(nx, nq, npar, 2, rfeat // 2)
    own_token = own_token.transpose(1, 3, 0, 2, 4).reshape(nz, 1, nx * npar, rfeat // 2)
    own_token = jnp.pad(own_token, ((0, 0), (0, 0), (0, 8 - own_token.shape[2]), (0, 0)))
    sent = to_tiles(own_cols)
    n_cols = sent.shape[0]
    sent = jnp.concatenate([jnp.broadcast_to(sent[None], (nz, n_cols, 8, 128)), own_token], axis=1)
    gathered = exchange(sent, LINE)
    half = from_tiles(gathered[:, :n_cols], tok).reshape(nz * tok, fcol)
    picked = gathered[:, n_cols, : nx * npar].reshape(nz // 8, 8, nx, npar, rfeat // 2)
    picked = picked.transpose(2, 3, 0, 1, 4)
    swap = [(0, 1), (1, 0)]
    own_weight = weight.T
    other_weight = lax.ppermute(own_weight, "xh", swap)

    halves = grad_in.reshape(2, tok, hid)
    from_a = lax.ppermute(jnp.where(xh == 0, halves[0], halves[1]), LEVEL, moves(0))
    from_b = lax.ppermute(jnp.where(xh == 0, halves[1], halves[0]), LEVEL, moves(1))
    own_first = core == xh
    cot = jnp.concatenate(
        [jnp.where(own_first, from_a, from_b), jnp.where(own_first, from_b, from_a)], axis=1
    )
    half, cot = lax.optimization_barrier((half, cot))

    both = jnp.concatenate([own_weight, other_weight], axis=0)
    part = lax.dot_general(half, both, (((1,), (1,)), ((), ())), preferred_element_type=jnp.float32)
    part = part.astype(jnp.bfloat16).reshape(ncol, tok, 2 * hid)
    pre_act = jnp.sum(exchange(part, COL).astype(jnp.float32), axis=0)
    slope = (cot.astype(jnp.float32) * silu_slope(pre_act)).astype(jnp.bfloat16)
    own, other = slope[:, :hid], slope[:, hid:]
    pair = jnp.concatenate([jnp.where(xh == 0, own, other), jnp.where(xh == 0, other, own)], axis=1)

    few = tok // npar
    pair = to_tiles(pair.reshape(npar, few, 2 * hid))
    sent = jnp.broadcast_to(pair[None], (nq, *pair.shape)).reshape(nz, -1, 8, 128)
    lines = exchange(sent, LINE)
    other_half = lax.ppermute(half, "xh", swap)
    lines, other_half = lax.optimization_barrier((lines, other_half))
    blocks = from_tiles(lines, few).reshape(nq, npar, few, 2 * hid)

    panels = jnp.stack(
        [
            jnp.concatenate([blocks[:, 0, :, :hid], blocks[:, 1, :, :hid]], axis=-1),
            jnp.concatenate([blocks[:, 0, :, hid:], blocks[:, 1, :, hid:]], axis=-1),
        ]
    )
    panels = to_tiles(panels.reshape(ncol, few, 2 * hid))
    rows = lax.dynamic_index_in_dim(blocks, lax.axis_index("zq"), 0, keepdims=False)
    rows = jnp.stack([rows[:, :, :hid], rows[:, :, hid:]])
    rows = to_tiles(jnp.pad(rows, ((0, 0), (0, 0), (0, 0), (0, LANES - hid))))
    n_panel, n_row = panels.shape[1], rows.shape[2]
    lead = (nx, npar, ncol)
    pieces = jnp.concatenate(
        [
            jnp.broadcast_to(panels, (nx, npar, *panels.shape)),
            jnp.broadcast_to(rows[:, :, None], (*lead, n_row, 8, 128)),
            jnp.broadcast_to(picked[:, :, None], (*lead, nz // 8, 8, 128)),
        ],
        axis=3,
    )
    pieces = exchange(pieces.reshape(nx * npar * ncol, -1, 8, 128), LEVELS)

    panel = from_tiles(pieces[:, :n_panel], few).reshape(-1, 2 * hid)
    row_block = from_tiles(pieces[:, n_panel : n_panel + n_row], few).reshape(-1, LANES)[:, :hid]
    grad_cov = dot(row_block, panel) / token_count

    cols = jnp.stack([jnp.where(xh == 0, half, other_half), jnp.where(xh == 0, other_half, half)])
    cols = cols.reshape(nx, nz, tok, fcol).transpose(0, 2, 1, 3).reshape(-1, fcol)
    act_rows = pieces[:, n_panel + n_row :].reshape(nx, npar, ncol, nz, rfeat // 2)
    act_rows = act_rows.transpose(0, 2, 3, 1, 4).reshape(-1, rfeat)
    act_cov = dot(act_rows, cols) / token_count
    return act_cov, grad_cov


def solution(mesh):
    fine = Mesh(mesh.devices.reshape(SIZES), AXES)
    placed = (P(ROW, None), P(COL, ROW), P(COL, ROW))
    return jax.shard_map(
        shards,
        mesh=fine,
        in_specs=placed,
        out_specs=(P(ROW, COL), P(ROW, COL)),
        check_vma=False,
    )
```

time: 124 us -> 118 us (0.952)
  blocking collectives: 28.6 us -> 17.9 us
  starting transfers between devices: 47.7 us -> 54.4 us
  waiting for transfers between devices: 36.5 us -> 34.2 us
    all_gather x1 -> x0, blocking collectives: 28.6 us -> none  [shards(): lines = lax.all_gather(sent, 'z', axis=0, tiled=False)]
    all_to_all x0 -> x1, blocking collectives: none -> 17.9 us  [exchange(): return lax.all_to_all(parts, axis, split_axis=0, concat_axis=0, tiled=True)]
    all_to_all x3, waiting for transfers between devices: 32.6 us -> 25.6 us  [exchange(): return lax.all_to_all(parts, axis, split_axis=0, concat_axis=0, tiled=True)]
    ppermute x1 -> x2, waiting for transfers between devices: 0.01 us -> 5.72 us  [the longest x1 5.72 us: shards(): other_half = lax.ppermute(half, 'xh', swap)]
    ppermute x1 -> x2, starting transfers between devices: 4.65 us -> 8.65 us  [the longest x1 4.65 us: shards(): other_weight = lax.ppermute(own_weight, 'xh', swap)]
    all_to_all x3, starting transfers between devices: 34.8 us -> 37.5 us  [exchange(): return lax.all_to_all(parts, axis, split_axis=0, concat_axis=0, tiled=True)]
    concatenate x4 -> x2, other arithmetic: 2.55 us -> 2.16 us  [the longest x1 1.42 us: shards(): jnp.concatenate([jnp.broadcast_to(panels, (nx, npar, *panels.shape)), jnp...]
  transfers between devices with their start and end apart: 6 -> 7, of which waited for: 3 -> 4; matrix products, arithmetic and copies ran while one was open for 1% -> 1% of each run, Pallas kernels for 0% -> 0%
where the time goes in v3:
time: 118 us; the launch traced here: 117 us
  starting transfers between devices  54.4 us (46%)
  waiting for transfers between devices  34.2 us (29%)
  blocking collectives  17.9 us (15%)
  other arithmetic  3.49 us (3%)
  matrix products  3.41 us (3%)
  local copies, waits for them, and re-layouts  2.91 us (2%)
    all_to_all x3, starting transfers between devices, exchange(): return lax.all_to_all(parts, axis, split_axis=0, concat_axis=0, tiled=True)  37.5 us
    all_to_all x3, waiting for transfers between devices, exchange(): return lax.all_to_all(parts, axis, split_axis=0, concat_axis=0, tiled=True)  25.6 us
    all_to_all x1, blocking collectives, exchange(): return lax.all_to_all(parts, axis, split_axis=0, concat_axis=0, tiled=True)  17.9 us
    ppermute x1, waiting for transfers between devices, shards(): other_half = lax.ppermute(half, 'xh', swap)  5.72 us
    ppermute x1, starting transfers between devices, shards(): other_weight = lax.ppermute(own_weight, 'xh', swap)  4.65 us
    ppermute x1, starting transfers between devices, shards(): lax.ppermute(jnp.where(xh == 0, halves[0], halves[1]), LEVEL, moves(0))  4.31 us
    ppermute x1, starting transfers between devices, shards(): other_half = lax.ppermute(half, 'xh', swap)  3.99 us
    ppermute x1, starting transfers between devices, shards(): lax.ppermute(jnp.where(xh == 0, halves[1], halves[0]), LEVEL, moves(1))  3.92 us
  transfers between devices with their start and end apart: 7, of which 4 were waited for; matrix products, arithmetic and copies ran while one was open for 1% of the time, Pallas kernels for 0%

profile of v3, /device:TPU:1, one launch (start us, length us, event | category | flops | bytes accessed | tf_op | source)
XLA Modules:
  0.0 117.2 jit_solution(11839315351273508476)
XLA Ops:
  0.6 0.0 copy-start
  0.6 0.0 copy-start.1
  0.7 0.9 copy-done
  1.6 0.1 dynamic-slice_reduce_fusion
  1.8 0.7 fusion.5
  2.5 15.7 %all-to-all-start = ((bf16[16,9,8,128]{3,2,1,0:T(8,128)(2,1)}), bf16[16,9,8,128]{3,2,1,0:T(8,128)(2,1)S(1)}, u32[]{:S(2)}, u32[]{:S(2)}) async-start(bf16[16,9,8,128]{3,2,1,0:T(8,128)(2,1)} %fusion.5), calls=%async_computation | async-start | bytes 589824 | tf_op jit(solution)/shard_map/all_to_all | solution.py:18
  18.3 4.7 %collective-permute-start.2 = (bf16[448,512]{1,0:T(8,128)(2,1)}, bf16[448,512]{1,0:T(8,128)(2,1)S(1)}, u32[]{:S(2)}, u32[]{:S(2)}) collective-permute-start(bf16[448,512]{1,0:T(8,128)(2,1)} %bitcast.111), channel_id=1, source_target_pairs={{0,256},{256,0},{1,257},{257,1},{2,258},{258,2},{3,259},{259,3},{4... | collective-permute-start | bytes 1376264 | tf_op jit(solution)/shard_map/ppermute | solution.py:78
  23.0 0.7 broadcast_select_fusion.7
  23.7 4.3 %collective-permute-start = (bf16[16,448]{1,0:T(8,128)(2,1)S(1)}, bf16[16,448]{1,0:T(8,128)(2,1)S(1)}, u32[]{:S(2)}, u32[]{:S(2)}) collective-permute-start(bf16[16,448]{1,0:T(8,128)(2,1)S(1)} %get-tuple-element.18), channel_id=1, source_target_pairs={{0,0},{1,2},{2,4},{3,6},{4,8},{5,10},{6,12},{7,14},{8,256},{9,258}... | collective-permute-start | bytes 43016 | tf_op jit(solution)/shard_map/ppermute | solution.py:81
  28.0 3.9 %collective-permute-start.1 = (bf16[16,448]{1,0:T(8,128)(2,1)S(1)}, bf16[16,448]{1,0:T(8,128)(2,1)S(1)}, u32[]{:S(2)}, u32[]{:S(2)}) collective-permute-start(bf16[16,448]{1,0:T(8,128)(2,1)S(1)} %get-tuple-element.19), channel_id=1, source_target_pairs={{0,1},{1,3},{2,5},{3,7},{4,9},{5,11},{6,13},{7,15},{8,257},{9,259}... | collective-permute-start | bytes 43016 | tf_op jit(solution)/shard_map/ppermute | solution.py:82
  32.0 2.8 %collective-permute-done = bf16[16,448]{1,0:T(8,128)(2,1)S(1)} collective-permute-done((bf16[16,448]{1,0:T(8,128)(2,1)S(1)}, bf16[16,448]{1,0:T(8,128)(2,1)S(1)}, u32[]{:S(2)}, u32[]{:S(2)}) %collective-permute-start) | collective-permute-done | bytes 14368 | tf_op jit(solution)/shard_map/ppermute | solution.py:81
  34.8 0.0 collective-permute-done.1
  34.8 0.1 pad_maximum_fusion.2
  34.9 0.0 all-to-all-done
  34.9 0.0 collective-permute-done.2
  34.9 0.0 copy-done.1
  34.9 0.5 convolution_convert_fusion
  35.4 17.9 %all_to_all.20 = bf16[16,16,896]{2,1,0:T(8,128)(2,1)S(1)} all-to-all(bf16[16,16,896]{2,1,0:T(8,128)(2,1)S(1)} %bitcast.106), channel_id=1, replica_groups=mesh['xh'=2,'zq'=8,'zp'=2,'xl'=2,'y'=4,'core'=2] {'xl','y','core'}, dimensions={0} | all-to-all | bytes 917504 | tf_op jit(solution)/shard_map/all_to_all | solution.py:18
  53.3 0.1 convert_reduce_fusion
  53.5 0.1 broadcast_select_fusion.5
  53.5 0.1 maximum_bitcast_fusion.3
  53.6 0.7 broadcast_in_dim.33
  54.3 9.5 %all-to-all-start.2 = ((bf16[16,7,8,128]{3,2,1,0:T(8,128)(2,1)}), bf16[16,7,8,128]{3,2,1,0:T(8,128)(2,1)S(1)}, u32[]{:S(2)}, u32[]{:S(2)}) async-start(bf16[16,7,8,128]{3,2,1,0:T(8,128)(2,1)} %bitcast.13), calls=%async_computation.2 | async-start | bytes 458752 | tf_op jit(solution)/shard_map/all_to_all | solution.py:18
  63.8 4.0 %collective-permute-start.3 = (bf16[256,512]{1,0:T(8,128)(2,1)S(1)}, bf16[256,512]{1,0:T(8,128)(2,1)S(1)}, u32[]{:S(2)}, u32[]{:S(2)}) collective-permute-start(bf16[256,512]{1,0:T(8,128)(2,1)S(1)} %bitcast.101), channel_id=1, source_target_pairs={{0,256},{256,0},{1,257},{257,1},{2,258},{258,2},{3,259},{259,3},{4... | collective-permute-start | bytes 786440 | tf_op jit(solution)/shard_map/ppermute | solution.py:101
  67.8 5.7 %collective-permute-done.3 = bf16[256,512]{1,0:T(8,128)(2,1)S(1)} collective-permute-done((bf16[256,512]{1,0:T(8,128)(2,1)S(1)}, bf16[256,512]{1,0:T(8,128)(2,1)S(1)}, u32[]{:S(2)}, u32[]{:S(2)}) %collective-permute-start.3) | collective-permute-done | bytes 262176 | tf_op jit(solution)/shard_map/ppermute | solution.py:101
  73.6 2.8 %all-to-all-done.2 = bf16[16,7,8,128]{3,2,1,0:T(8,128)(2,1)S(1)} async-done(((bf16[16,7,8,128]{3,2,1,0:T(8,128)(2,1)}), bf16[16,7,8,128]{3,2,1,0:T(8,128)(2,1)S(1)}, u32[]{:S(2)}, u32[]{:S(2)}) %all-to-all-start.2) | async-done | bytes 229408 | tf_op jit(solution)/shard_map/all_to_all | solution.py:18
  76.4 0.1 slice_bitcast_fusion.6
  76.5 0.1 slice_bitcast_fusion.8
  76.6 0.1 maximum_bitcast_fusion.1
  76.8 0.1 broadcast_in_dim.36
  76.9 0.1 broadcast_in_dim.34
  77.0 1.4 %pad_maximum_fusion = bf16[2,2,16,13,8,128]{5,4,3,2,1,0:T(8,128)(2,1)} fusion(bf16[2,2,16,2,8,128]{5,4,3,2,1,0:T(8,128)(2,1)S(1)} %broadcast_in_dim.37, bf16[2,2,16,4,8,128]{5,4,3,2,1,0:T(8,128)(2,1)S(1)} %broadcast_in_dim.36, bf16[2,2,16,7,8,128]{5,4,3,2,1,0:T(8,128)(2,1)S(1)} %broadcast_in_dim.34), kind=kLoop, calls=%fused_computation | loop fusion | flops 1703936 | bytes 3407872 | tf_op jit(solution)/shard_map/concatenate | solution.py:117
  78.4 12.3 %all-to-all-start.3 = ((bf16[64,13,8,128]{3,2,1,0:T(8,128)(2,1)}), bf16[64,13,8,128]{3,2,1,0:T(8,128)(2,1)S(1)}, u32[]{:S(2)}, u32[]{:S(2)}) async-start(bf16[64,13,8,128]{3,2,1,0:T(8,128)(2,1)} %bitcast.36), calls=%async_computation.3 | async-start | bytes 3407872 | tf_op jit(solution)/shard_map/all_to_all | solution.py:18
  90.8 0.1 maximum_bitcast_fusion
  90.9 0.3 copy.21
  91.2 22.8 %all-to-all-done.3 = bf16[64,13,8,128]{3,2,1,0:T(8,128)(2,1)S(1)} async-done(((bf16[64,13,8,128]{3,2,1,0:T(8,128)(2,1)}), bf16[64,13,8,128]{3,2,1,0:T(8,128)(2,1)S(1)}, u32[]{:S(2)}, u32[]{:S(2)}) %all-to-all-start.3) | async-done | bytes 1703968 | tf_op jit(solution)/shard_map/all_to_all | solution.py:18
  114.0 0.3 copy.20
  114.3 1.1 convolution_multiply_fusion.1
  115.4 1.8 %convolution_multiply_fusion = f32[448,896]{1,0:T(8,128)} fusion(bf16[64,13,8,128]{3,2,1,0:T(8,128)(2,1)S(1)} %all-to-all-done.3, bf16[512,512]{1,0:T(8,128)(2,1)S(1)} %slice_bitcast_fusion.2), kind=kOutput, calls=%fused_computation.1 | convolution fusion | flops 411443200 | bytes 3047424 | tf_op jit(solution)/shard_map/dot_general | solution.py:27
  (16 shorter events, 0.3 us)
Async XLA Ops:
  0.6 1.0 copy-start
  0.6 34.3 %copy-start.1 = (bf16[512,448]{0,1:T(8,128)(2,1)S(1)}, bf16[512,448]{0,1:T(8,128)(2,1)}, u32[]{:S(2)}) copy-start(bf16[512,448]{0,1:T(8,128)(2,1)} %param.4) | copy-start | bytes 1376260
  2.5 32.3 %all-to-all-start = ((bf16[16,9,8,128]{3,2,1,0:T(8,128)(2,1)}), bf16[16,9,8,128]{3,2,1,0:T(8,128)(2,1)S(1)}, u32[]{:S(2)}, u32[]{:S(2)}) async-start(bf16[16,9,8,128]{3,2,1,0:T(8,128)(2,1)} %fusion.5), calls=%async_computation | async-start | bytes 589824 | tf_op jit(solution)/shard_map/all_to_all | solution.py:18
  18.3 16.6 %collective-permute-start.2 = (bf16[448,512]{1,0:T(8,128)(2,1)}, bf16[448,512]{1,0:T(8,128)(2,1)S(1)}, u32[]{:S(2)}, u32[]{:S(2)}) collective-permute-start(bf16[448,512]{1,0:T(8,128)(2,1)} %bitcast.111), channel_id=1, source_target_pairs={{0,256},{256,0},{1,257},{257,1},{2,258},{258,2},{3,259},{259,3},{4... | collective-permute-start | bytes 1376264 | tf_op jit(solution)/shard_map/ppermute | solution.py:78
  23.7 11.1 %collective-permute-start = (bf16[16,448]{1,0:T(8,128)(2,1)S(1)}, bf16[16,448]{1,0:T(8,128)(2,1)S(1)}, u32[]{:S(2)}, u32[]{:S(2)}) collective-permute-start(bf16[16,448]{1,0:T(8,128)(2,1)S(1)} %get-tuple-element.18), channel_id=1, source_target_pairs={{0,0},{1,2},{2,4},{3,6},{4,8},{5,10},{6,12},{7,14},{8,256},{9,258}... | collective-permute-start | bytes 43016 | tf_op jit(solution)/shard_map/ppermute | solution.py:81
  28.0 6.8 %collective-permute-start.1 = (bf16[16,448]{1,0:T(8,128)(2,1)S(1)}, bf16[16,448]{1,0:T(8,128)(2,1)S(1)}, u32[]{:S(2)}, u32[]{:S(2)}) collective-permute-start(bf16[16,448]{1,0:T(8,128)(2,1)S(1)} %get-tuple-element.19), channel_id=1, source_target_pairs={{0,1},{1,3},{2,5},{3,7},{4,9},{5,11},{6,13},{7,15},{8,257},{9,259}... | collective-permute-start | bytes 43016 | tf_op jit(solution)/shard_map/ppermute | solution.py:82
  54.3 22.1 %all-to-all-start.2 = ((bf16[16,7,8,128]{3,2,1,0:T(8,128)(2,1)}), bf16[16,7,8,128]{3,2,1,0:T(8,128)(2,1)S(1)}, u32[]{:S(2)}, u32[]{:S(2)}) async-start(bf16[16,7,8,128]{3,2,1,0:T(8,128)(2,1)} %bitcast.13), calls=%async_computation.2 | async-start | bytes 458752 | tf_op jit(solution)/shard_map/all_to_all | solution.py:18
  63.8 9.7 %collective-permute-start.3 = (bf16[256,512]{1,0:T(8,128)(2,1)S(1)}, bf16[256,512]{1,0:T(8,128)(2,1)S(1)}, u32[]{:S(2)}, u32[]{:S(2)}) collective-permute-start(bf16[256,512]{1,0:T(8,128)(2,1)S(1)} %bitcast.101), channel_id=1, source_target_pairs={{0,256},{256,0},{1,257},{257,1},{2,258},{258,2},{3,259},{259,3},{4... | collective-permute-start | bytes 786440 | tf_op jit(solution)/shard_map/ppermute | solution.py:101
  78.4 35.5 %all-to-all-start.3 = ((bf16[64,13,8,128]{3,2,1,0:T(8,128)(2,1)}), bf16[64,13,8,128]{3,2,1,0:T(8,128)(2,1)S(1)}, u32[]{:S(2)}, u32[]{:S(2)}) async-start(bf16[64,13,8,128]{3,2,1,0:T(8,128)(2,1)} %bitcast.36), calls=%async_computation.3 | async-start | bytes 3407872 | tf_op jit(solution)/shard_map/all_to_all | solution.py:18

commit v4 on v3

--- a/solution.py
+++ b/solution.py
@@ -99,7 +99,9 @@
     sent = jnp.broadcast_to(pair[None], (nq, *pair.shape)).reshape(nz, -1, 8, 128)
     lines = exchange(sent, LINE)
     other_half = lax.ppermute(half, "xh", swap)
-    lines, other_half = lax.optimization_barrier((lines, other_half))
+    cols = jnp.stack([jnp.where(xh == 0, half, other_half), jnp.where(xh == 0, other_half, half)])
+    cols = cols.reshape(nx, nz, tok, fcol).transpose(0, 2, 1, 3).reshape(-1, fcol)
+    lines, cols = lax.optimization_barrier((lines, cols))
     blocks = from_tiles(lines, few).reshape(nq, npar, few, 2 * hid)
 
     panels = jnp.stack(
@@ -128,8 +130,6 @@
     row_block = from_tiles(pieces[:, n_panel : n_panel + n_row], few).reshape(-1, LANES)[:, :hid]
     grad_cov = dot(row_block, panel) / token_count
 
-    cols = jnp.stack([jnp.where(xh == 0, half, other_half), jnp.where(xh == 0, other_half, half)])
-    cols = cols.reshape(nx, nz, tok, fcol).transpose(0, 2, 1, 3).reshape(-1, fcol)
     act_rows = pieces[:, n_panel + n_row :].reshape(nx, npar, ncol, nz, rfeat // 2)
     act_rows = act_rows.transpose(0, 2, 3, 1, 4).reshape(-1, rfeat)
     act_cov = dot(act_rows, cols) / token_count

time: 118 us -> 117 us (level)
  blocking collectives: 17.9 us -> 53.2 us
  waiting for transfers between devices: 34.2 us -> 11 us
  starting transfers between devices: 54.4 us -> 42.1 us
  other arithmetic: 3.49 us -> 2.27 us
    all_to_all x1 -> x2, blocking collectives: 17.9 us -> 53.2 us  [exchange(): return lax.all_to_all(parts, axis, split_axis=0, concat_axis=0, tiled=True)]
    all_to_all x3 -> x2, waiting for transfers between devices: 25.6 us -> 2.45 us  [exchange(): return lax.all_to_all(parts, axis, split_axis=0, concat_axis=0, tiled=True)]
    all_to_all x3 -> x2, starting transfers between devices: 37.5 us -> 25.2 us  [exchange(): return lax.all_to_all(parts, axis, split_axis=0, concat_axis=0, tiled=True)]
    concatenate x1, other arithmetic: 1.42 us -> 0.2 us  [shards(): jnp.concatenate([jnp.broadcast_to(panels, (nx, npar, *panels.shape)), jnp...]
  transfers between devices with their start and end apart: 7 -> 6, of which waited for: 4 -> 3; matrix products, arithmetic and copies ran while one was open for 1% -> 1% of each run, Pallas kernels for 0% -> 0%
where the time goes in v4:
time: 117 us; the launch traced here: 116 us
  blocking collectives  53.2 us (45%)
  starting transfers between devices  42.1 us (36%)
  waiting for transfers between devices  11 us (9%)
  matrix products  3.42 us (3%)
  local copies, waits for them, and re-layouts  2.91 us (2%)
  other arithmetic  2.27 us (2%)
    all_to_all x2, blocking collectives, exchange(): return lax.all_to_all(parts, axis, split_axis=0, concat_axis=0, tiled=True)  53.2 us
    all_to_all x2, starting transfers between devices, exchange(): return lax.all_to_all(parts, axis, split_axis=0, concat_axis=0, tiled=True)  25.2 us
    ppermute x1, waiting for transfers between devices, shards(): other_half = lax.ppermute(half, 'xh', swap)  5.72 us
    ppermute x1, starting transfers between devices, shards(): other_weight = lax.ppermute(own_weight, 'xh', swap)  4.65 us
    ppermute x1, starting transfers between devices, shards(): lax.ppermute(jnp.where(xh == 0, halves[0], halves[1]), LEVEL, moves(0))  4.31 us
    ppermute x1, starting transfers between devices, shards(): other_half = lax.ppermute(half, 'xh', swap)  3.99 us
    ppermute x1, starting transfers between devices, shards(): lax.ppermute(jnp.where(xh == 0, halves[1], halves[0]), LEVEL, moves(1))  3.92 us
    dot_general x2, matrix products, dot(): return lax.dot_general(a, b, CONTRACT, preferred_element_type=jnp.float32)  2.95 us
  transfers between devices with their start and end apart: 6, of which 3 were waited for; matrix products, arithmetic and copies ran while one was open for 1% of the time, Pallas kernels for 0%

profile of v4, /device:TPU:1, one launch (start us, length us, event | category | flops | bytes accessed | tf_op | source)
XLA Modules:
  0.0 115.8 jit_solution(2427161378577760755)
XLA Ops:
  0.6 0.0 copy-start
  0.6 0.0 copy-start.1
  0.7 0.9 copy-done
  1.6 0.1 dynamic-slice_reduce_fusion
  1.8 0.7 fusion.5
  2.5 15.7 %all-to-all-start = ((bf16[16,9,8,128]{3,2,1,0:T(8,128)(2,1)}), bf16[16,9,8,128]{3,2,1,0:T(8,128)(2,1)S(1)}, u32[]{:S(2)}, u32[]{:S(2)}) async-start(bf16[16,9,8,128]{3,2,1,0:T(8,128)(2,1)} %fusion.5), calls=%async_computation | async-start | bytes 589824 | tf_op jit(solution)/shard_map/all_to_all | solution.py:18
  18.3 4.7 %collective-permute-start.2 = (bf16[448,512]{1,0:T(8,128)(2,1)}, bf16[448,512]{1,0:T(8,128)(2,1)S(1)}, u32[]{:S(2)}, u32[]{:S(2)}) collective-permute-start(bf16[448,512]{1,0:T(8,128)(2,1)} %bitcast.114), channel_id=1, source_target_pairs={{0,256},{256,0},{1,257},{257,1},{2,258},{258,2},{3,259},{259,3},{4... | collective-permute-start | bytes 1376264 | tf_op jit(solution)/shard_map/ppermute | solution.py:78
  23.0 0.7 broadcast_select_fusion.7
  23.7 4.3 %collective-permute-start = (bf16[16,448]{1,0:T(8,128)(2,1)S(1)}, bf16[16,448]{1,0:T(8,128)(2,1)S(1)}, u32[]{:S(2)}, u32[]{:S(2)}) collective-permute-start(bf16[16,448]{1,0:T(8,128)(2,1)S(1)} %get-tuple-element.18), channel_id=1, source_target_pairs={{0,0},{1,2},{2,4},{3,6},{4,8},{5,10},{6,12},{7,14},{8,256},{9,258}... | collective-permute-start | bytes 43016 | tf_op jit(solution)/shard_map/ppermute | solution.py:81
  28.0 3.9 %collective-permute-start.1 = (bf16[16,448]{1,0:T(8,128)(2,1)S(1)}, bf16[16,448]{1,0:T(8,128)(2,1)S(1)}, u32[]{:S(2)}, u32[]{:S(2)}) collective-permute-start(bf16[16,448]{1,0:T(8,128)(2,1)S(1)} %get-tuple-element.19), channel_id=1, source_target_pairs={{0,1},{1,3},{2,5},{3,7},{4,9},{5,11},{6,13},{7,15},{8,257},{9,259}... | collective-permute-start | bytes 43016 | tf_op jit(solution)/shard_map/ppermute | solution.py:82
  32.0 2.8 %collective-permute-done = bf16[16,448]{1,0:T(8,128)(2,1)S(1)} collective-permute-done((bf16[16,448]{1,0:T(8,128)(2,1)S(1)}, bf16[16,448]{1,0:T(8,128)(2,1)S(1)}, u32[]{:S(2)}, u32[]{:S(2)}) %collective-permute-start) | collective-permute-done | bytes 14368 | tf_op jit(solution)/shard_map/ppermute | solution.py:81
  34.8 0.0 collective-permute-done.1
  34.8 0.1 pad_maximum_fusion.2
  34.9 0.0 all-to-all-done
  34.9 0.0 collective-permute-done.2
  34.9 0.0 copy-done.1
  34.9 0.5 convolution_convert_fusion
  35.4 17.9 %all_to_all.20 = bf16[16,16,896]{2,1,0:T(8,128)(2,1)S(1)} all-to-all(bf16[16,16,896]{2,1,0:T(8,128)(2,1)S(1)} %bitcast.108), channel_id=1, replica_groups=mesh['xh'=2,'zq'=8,'zp'=2,'xl'=2,'y'=4,'core'=2] {'xl','y','core'}, dimensions={0} | all-to-all | bytes 917504 | tf_op jit(solution)/shard_map/all_to_all | solution.py:18
  53.3 0.1 convert_reduce_fusion
  53.5 0.1 broadcast_select_fusion.5
  53.5 0.1 maximum_bitcast_fusion.3
  53.6 0.7 broadcast_in_dim.33
  54.3 9.5 %all-to-all-start.2 = ((bf16[16,7,8,128]{3,2,1,0:T(8,128)(2,1)}), bf16[16,7,8,128]{3,2,1,0:T(8,128)(2,1)S(1)}, u32[]{:S(2)}, u32[]{:S(2)}) async-start(bf16[16,7,8,128]{3,2,1,0:T(8,128)(2,1)} %bitcast.13), calls=%async_computation.2 | async-start | bytes 458752 | tf_op jit(solution)/shard_map/all_to_all | solution.py:18
  63.8 4.0 %collective-permute-start.3 = (bf16[256,512]{1,0:T(8,128)(2,1)S(1)}, bf16[256,512]{1,0:T(8,128)(2,1)S(1)}, u32[]{:S(2)}, u32[]{:S(2)}) collective-permute-start(bf16[256,512]{1,0:T(8,128)(2,1)S(1)} %bitcast.103), channel_id=1, source_target_pairs={{0,256},{256,0},{1,257},{257,1},{2,258},{258,2},{3,259},{259,3},{4... | collective-permute-start | bytes 786440 | tf_op jit(solution)/shard_map/ppermute | solution.py:101
  67.8 5.7 %collective-permute-done.3 = bf16[256,512]{1,0:T(8,128)(2,1)S(1)} collective-permute-done((bf16[256,512]{1,0:T(8,128)(2,1)S(1)}, bf16[256,512]{1,0:T(8,128)(2,1)S(1)}, u32[]{:S(2)}, u32[]{:S(2)}) %collective-permute-start.3) | collective-permute-done | bytes 262176 | tf_op jit(solution)/shard_map/ppermute | solution.py:101
  73.6 0.1 maximum_bitcast_fusion
  73.7 0.3 copy.16
  74.0 2.4 %all-to-all-done.2 = bf16[16,7,8,128]{3,2,1,0:T(8,128)(2,1)S(1)} async-done(((bf16[16,7,8,128]{3,2,1,0:T(8,128)(2,1)}), bf16[16,7,8,128]{3,2,1,0:T(8,128)(2,1)S(1)}, u32[]{:S(2)}, u32[]{:S(2)}) %all-to-all-start.2) | async-done | bytes 229408 | tf_op jit(solution)/shard_map/all_to_all | solution.py:18
  76.4 0.1 slice_bitcast_fusion.6
  76.5 0.1 slice_bitcast_fusion.8
  76.6 0.1 maximum_bitcast_fusion.1
  76.8 0.1 broadcast_in_dim.36
  76.9 0.1 broadcast_in_dim.34
  77.0 0.2 pad_maximum_fusion
  77.2 35.3 %all_to_all.21 = bf16[64,13,8,128]{3,2,1,0:T(8,128)(2,1)S(1)} all-to-all(bf16[64,13,8,128]{3,2,1,0:T(8,128)(2,1)S(1)} %bitcast.96), channel_id=1, replica_groups=mesh['xh'=2,'zq'=8,'zp'=2,'xl'=2,'y'=4,'core'=2] {'xh','zp','xl','y','co..., dimensions={0} | all-to-all | bytes 3407872 | tf_op jit(solution)/shard_map/all_to_all | solution.py:18
  112.6 0.3 copy.21
  112.8 1.1 convolution_multiply_fusion.1
  114.0 1.8 %convolution_multiply_fusion = f32[448,896]{1,0:T(8,128)} fusion(bf16[64,13,8,128]{3,2,1,0:T(8,128)(2,1)S(1)} %all_to_all.21, bf16[512,512]{1,0:T(8,128)(2,1)S(1)} %slice_bitcast_fusion.2), kind=kOutput, calls=%fused_computation.1 | convolution fusion | flops 411443200 | bytes 3047424 | tf_op jit(solution)/shard_map/dot_general | solution.py:27
  (16 shorter events, 0.3 us)
Async XLA Ops:
  0.6 1.0 copy-start
  0.6 34.3 %copy-start.1 = (bf16[512,448]{0,1:T(8,128)(2,1)S(1)}, bf16[512,448]{0,1:T(8,128)(2,1)}, u32[]{:S(2)}) copy-start(bf16[512,448]{0,1:T(8,128)(2,1)} %param.4) | copy-start | bytes 1376260
  2.5 32.3 %all-to-all-start = ((bf16[16,9,8,128]{3,2,1,0:T(8,128)(2,1)}), bf16[16,9,8,128]{3,2,1,0:T(8,128)(2,1)S(1)}, u32[]{:S(2)}, u32[]{:S(2)}) async-start(bf16[16,9,8,128]{3,2,1,0:T(8,128)(2,1)} %fusion.5), calls=%async_computation | async-start | bytes 589824 | tf_op jit(solution)/shard_map/all_to_all | solution.py:18
  18.3 16.6 %collective-permute-start.2 = (bf16[448,512]{1,0:T(8,128)(2,1)}, bf16[448,512]{1,0:T(8,128)(2,1)S(1)}, u32[]{:S(2)}, u32[]{:S(2)}) collective-permute-start(bf16[448,512]{1,0:T(8,128)(2,1)} %bitcast.114), channel_id=1, source_target_pairs={{0,256},{256,0},{1,257},{257,1},{2,258},{258,2},{3,259},{259,3},{4... | collective-permute-start | bytes 1376264 | tf_op jit(solution)/shard_map/ppermute | solution.py:78
  23.7 11.1 %collective-permute-start = (bf16[16,448]{1,0:T(8,128)(2,1)S(1)}, bf16[16,448]{1,0:T(8,128)(2,1)S(1)}, u32[]{:S(2)}, u32[]{:S(2)}) collective-permute-start(bf16[16,448]{1,0:T(8,128)(2,1)S(1)} %get-tuple-element.18), channel_id=1, source_target_pairs={{0,0},{1,2},{2,4},{3,6},{4,8},{5,10},{6,12},{7,14},{8,256},{9,258}... | collective-permute-start | bytes 43016 | tf_op jit(solution)/shard_map/ppermute | solution.py:81
  28.0 6.8 %collective-permute-start.1 = (bf16[16,448]{1,0:T(8,128)(2,1)S(1)}, bf16[16,448]{1,0:T(8,128)(2,1)S(1)}, u32[]{:S(2)}, u32[]{:S(2)}) collective-permute-start(bf16[16,448]{1,0:T(8,128)(2,1)S(1)} %get-tuple-element.19), channel_id=1, source_target_pairs={{0,1},{1,3},{2,5},{3,7},{4,9},{5,11},{6,13},{7,15},{8,257},{9,259}... | collective-permute-start | bytes 43016 | tf_op jit(solution)/shard_map/ppermute | solution.py:82
  54.3 22.1 %all-to-all-start.2 = ((bf16[16,7,8,128]{3,2,1,0:T(8,128)(2,1)}), bf16[16,7,8,128]{3,2,1,0:T(8,128)(2,1)S(1)}, u32[]{:S(2)}, u32[]{:S(2)}) async-start(bf16[16,7,8,128]{3,2,1,0:T(8,128)(2,1)} %bitcast.13), calls=%async_computation.2 | async-start | bytes 458752 | tf_op jit(solution)/shard_map/all_to_all | solution.py:18
  63.8 9.7 %collective-permute-start.3 = (bf16[256,512]{1,0:T(8,128)(2,1)S(1)}, bf16[256,512]{1,0:T(8,128)(2,1)S(1)}, u32[]{:S(2)}, u32[]{:S(2)}) collective-permute-start(bf16[256,512]{1,0:T(8,128)(2,1)S(1)} %bitcast.103), channel_id=1, source_target_pairs={{0,256},{256,0},{1,257},{257,1},{2,258},{258,2},{3,259},{259,3},{4... | collective-permute-start | bytes 786440 | tf_op jit(solution)/shard_map/ppermute | solution.py:101

commit v5 on v4

--- a/solution.py
+++ b/solution.py
@@ -1,6 +1,10 @@
+import functools
+
 import jax
 import jax.numpy as jnp
 from jax import lax
+from jax.experimental import pallas as pl
+from jax.experimental.pallas import tpu as pltpu
 from jax.sharding import Mesh, PartitionSpec as P
 
 AXES = ("xh", "zq", "zp", "xl", "y", "core")
@@ -25,6 +29,37 @@
 
 def dot(a, b):
     return lax.dot_general(a, b, CONTRACT, preferred_element_type=jnp.float32)
+
+
+def covariance_kernel(scale, rows_ref, panel_ref, act_rows_ref, cols_ref, grad_ref, act_ref, rows_t, act_t):
+    step = pl.program_id(0)
+
+    @pl.when(step == 0)
+    def _():
+        rows_t[...] = rows_ref[...].T
+        act_t[...] = act_rows_ref[...].T
+
+    for left, right, out in ((rows_t, panel_ref, grad_ref), (act_t, cols_ref, act_ref)):
+        count = out.shape[0]
+        mine = left[pl.ds(pl.multiple_of(step * count, count), count), :]
+        out[...] = jnp.dot(mine, right[...], preferred_element_type=jnp.float32) * scale
+
+
+def covariances(rows, panel, act_rows, cols, height, scale):
+    steps = 2
+    outs = [(height, panel.shape[1]), (act_rows.shape[1], cols.shape[1])]
+    return pl.pallas_call(
+        functools.partial(covariance_kernel, scale),
+        grid=(steps,),
+        in_specs=[pl.BlockSpec(memory_space=pltpu.VMEM)] * 4,
+        out_specs=[pl.BlockSpec((m // steps, n), lambda i: (i, 0)) for m, n in outs],
+        out_shape=[jax.ShapeDtypeStruct(shape, jnp.float32) for shape in outs],
+        scratch_shapes=[
+            pltpu.VMEM(rows.shape[::-1], rows.dtype),
+            pltpu.VMEM(act_rows.shape[::-1], act_rows.dtype),
+        ],
+        compiler_params=pltpu.CompilerParams(vmem_limit_bytes=16 * 1024 * 1024),
+    )(rows, panel, act_rows, cols)
 
 
 def to_tiles(x):
@@ -127,12 +162,10 @@
     pieces = exchange(pieces.reshape(nx * npar * ncol, -1, 8, 128), LEVELS)
 
     panel = from_tiles(pieces[:, :n_panel], few).reshape(-1, 2 * hid)
-    row_block = from_tiles(pieces[:, n_panel : n_panel + n_row], few).reshape(-1, LANES)[:, :hid]
-    grad_cov = dot(row_block, panel) / token_count
-
+    row_block = from_tiles(pieces[:, n_panel : n_panel + n_row], few).reshape(-1, LANES)
     act_rows = pieces[:, n_panel + n_row :].reshape(nx, npar, ncol, nz, rfeat // 2)
     act_rows = act_rows.transpose(0, 2, 3, 1, 4).reshape(-1, rfeat)
-    act_cov = dot(act_rows, cols) / token_count
+    grad_cov, act_cov = covariances(row_block, panel, act_rows, cols, hid, 1.0 / token_count)
     return act_cov, grad_cov
 
 

time: 117 us -> 116 us (level)
  matrix products: 3.42 us -> 0.47 us
  Pallas kernels: 0 us -> 2.15 us
    dot_general x2 -> x0, matrix products: 2.95 us -> none  [dot(): return lax.dot_general(a, b, CONTRACT, preferred_element_type=jnp.float32)]
    pallas_call x0 -> x1, Pallas kernels: none -> 2.15 us  [covariances(): pl.pallas_call(functools.partial(covariance_kernel, scale), grid=(steps,)...]
where the time goes in v5:
time: 116 us; the launch traced here: 115 us
  blocking collectives  53.2 us (46%)
  starting transfers between devices  42.1 us (36%)
  waiting for transfers between devices  11 us (9%)
  local copies, waits for them, and re-layouts  3.03 us (3%)
  other arithmetic  2.27 us (2%)
  Pallas kernels  2.15 us (2%)
    all_to_all x2, blocking collectives, exchange(): return lax.all_to_all(parts, axis, split_axis=0, concat_axis=0, tiled=True)  53.2 us
    all_to_all x2, starting transfers between devices, exchange(): return lax.all_to_all(parts, axis, split_axis=0, concat_axis=0, tiled=True)  25.2 us
    ppermute x1, waiting for transfers between devices, shards(): other_half = lax.ppermute(half, 'xh', swap)  5.72 us
    ppermute x1, starting transfers between devices, shards(): other_weight = lax.ppermute(own_weight, 'xh', swap)  4.65 us
    ppermute x1, starting transfers between devices, shards(): lax.ppermute(jnp.where(xh == 0, halves[0], halves[1]), LEVEL, moves(0))  4.31 us
    ppermute x1, starting transfers between devices, shards(): other_half = lax.ppermute(half, 'xh', swap)  3.99 us
    ppermute x1, starting transfers between devices, shards(): lax.ppermute(jnp.where(xh == 0, halves[1], halves[0]), LEVEL, moves(1))  3.92 us
    ppermute x1, waiting for transfers between devices, shards(): lax.ppermute(jnp.where(xh == 0, halves[0], halves[1]), LEVEL, moves(0))  2.83 us
  transfers between devices with their start and end apart: 6, of which 3 were waited for; matrix products, arithmetic and copies ran while one was open for 1% of the time, Pallas kernels for 0%

profile of v5, /device:TPU:1, one launch (start us, length us, event | category | flops | bytes accessed | tf_op | source)
XLA Modules:
  0.0 115.2 jit_solution(5055193197266661138)
XLA Ops:
  0.6 0.0 copy-start
  0.6 0.0 copy-start.1
  0.7 0.9 copy-done
  1.6 0.1 dynamic-slice_reduce_fusion
  1.8 0.7 fusion.4
  2.5 15.7 %all-to-all-start = ((bf16[16,9,8,128]{3,2,1,0:T(8,128)(2,1)}), bf16[16,9,8,128]{3,2,1,0:T(8,128)(2,1)S(1)}, u32[]{:S(2)}, u32[]{:S(2)}) async-start(bf16[16,9,8,128]{3,2,1,0:T(8,128)(2,1)} %fusion.4), calls=%async_computation | async-start | bytes 589824 | tf_op jit(solution)/shard_map/all_to_all | solution.py:22
  18.3 4.7 %collective-permute-start.2 = (bf16[448,512]{1,0:T(8,128)(2,1)}, bf16[448,512]{1,0:T(8,128)(2,1)S(1)}, u32[]{:S(2)}, u32[]{:S(2)}) collective-permute-start(bf16[448,512]{1,0:T(8,128)(2,1)} %bitcast.111), channel_id=1, source_target_pairs={{0,256},{256,0},{1,257},{257,1},{2,258},{258,2},{3,259},{259,3},{4... | collective-permute-start | bytes 1376264 | tf_op jit(solution)/shard_map/ppermute | solution.py:113
  23.0 0.7 broadcast_select_fusion.7
  23.7 4.3 %collective-permute-start = (bf16[16,448]{1,0:T(8,128)(2,1)S(1)}, bf16[16,448]{1,0:T(8,128)(2,1)S(1)}, u32[]{:S(2)}, u32[]{:S(2)}) collective-permute-start(bf16[16,448]{1,0:T(8,128)(2,1)S(1)} %get-tuple-element.22), channel_id=1, source_target_pairs={{0,0},{1,2},{2,4},{3,6},{4,8},{5,10},{6,12},{7,14},{8,256},{9,258}... | collective-permute-start | bytes 43016 | tf_op jit(solution)/shard_map/ppermute | solution.py:116
  28.0 3.9 %collective-permute-start.1 = (bf16[16,448]{1,0:T(8,128)(2,1)S(1)}, bf16[16,448]{1,0:T(8,128)(2,1)S(1)}, u32[]{:S(2)}, u32[]{:S(2)}) collective-permute-start(bf16[16,448]{1,0:T(8,128)(2,1)S(1)} %get-tuple-element.23), channel_id=1, source_target_pairs={{0,1},{1,3},{2,5},{3,7},{4,9},{5,11},{6,13},{7,15},{8,257},{9,259}... | collective-permute-start | bytes 43016 | tf_op jit(solution)/shard_map/ppermute | solution.py:117
  32.0 2.8 %collective-permute-done = bf16[16,448]{1,0:T(8,128)(2,1)S(1)} collective-permute-done((bf16[16,448]{1,0:T(8,128)(2,1)S(1)}, bf16[16,448]{1,0:T(8,128)(2,1)S(1)}, u32[]{:S(2)}, u32[]{:S(2)}) %collective-permute-start) | collective-permute-done | bytes 14368 | tf_op jit(solution)/shard_map/ppermute | solution.py:116
  34.8 0.0 collective-permute-done.1
  34.8 0.1 pad_maximum_fusion.2
  34.9 0.0 all-to-all-done
  34.9 0.0 collective-permute-done.2
  34.9 0.0 copy-done.1
  34.9 0.5 convolution_convert_fusion
  35.4 17.9 %all_to_all.20 = bf16[16,16,896]{2,1,0:T(8,128)(2,1)S(1)} all-to-all(bf16[16,16,896]{2,1,0:T(8,128)(2,1)S(1)} %bitcast.106), channel_id=1, replica_groups=mesh['xh'=2,'zq'=8,'zp'=2,'xl'=2,'y'=4,'core'=2] {'xl','y','core'}, dimensions={0} | all-to-all | bytes 917504 | tf_op jit(solution)/shard_map/all_to_all | solution.py:22
  53.3 0.1 convert_reduce_fusion
  53.5 0.1 broadcast_select_fusion.5
  53.5 0.1 maximum_bitcast_fusion.3
  53.6 0.7 broadcast_in_dim.33
  54.3 9.5 %all-to-all-start.2 = ((bf16[16,7,8,128]{3,2,1,0:T(8,128)(2,1)}), bf16[16,7,8,128]{3,2,1,0:T(8,128)(2,1)S(1)}, u32[]{:S(2)}, u32[]{:S(2)}) async-start(bf16[16,7,8,128]{3,2,1,0:T(8,128)(2,1)} %bitcast.13), calls=%async_computation.2 | async-start | bytes 458752 | tf_op jit(solution)/shard_map/all_to_all | solution.py:22
  63.8 4.0 %collective-permute-start.3 = (bf16[256,512]{1,0:T(8,128)(2,1)S(1)}, bf16[256,512]{1,0:T(8,128)(2,1)S(1)}, u32[]{:S(2)}, u32[]{:S(2)}) collective-permute-start(bf16[256,512]{1,0:T(8,128)(2,1)S(1)} %bitcast.101), channel_id=1, source_target_pairs={{0,256},{256,0},{1,257},{257,1},{2,258},{258,2},{3,259},{259,3},{4... | collective-permute-start | bytes 786440 | tf_op jit(solution)/shard_map/ppermute | solution.py:136
  67.8 5.7 %collective-permute-done.3 = bf16[256,512]{1,0:T(8,128)(2,1)S(1)} collective-permute-done((bf16[256,512]{1,0:T(8,128)(2,1)S(1)}, bf16[256,512]{1,0:T(8,128)(2,1)S(1)}, u32[]{:S(2)}, u32[]{:S(2)}) %collective-permute-start.3) | collective-permute-done | bytes 262176 | tf_op jit(solution)/shard_map/ppermute | solution.py:136
  73.6 0.1 maximum_bitcast_fusion
  73.7 0.3 copy.17
  74.0 2.4 %all-to-all-done.2 = bf16[16,7,8,128]{3,2,1,0:T(8,128)(2,1)S(1)} async-done(((bf16[16,7,8,128]{3,2,1,0:T(8,128)(2,1)}), bf16[16,7,8,128]{3,2,1,0:T(8,128)(2,1)S(1)}, u32[]{:S(2)}, u32[]{:S(2)}) %all-to-all-start.2) | async-done | bytes 229408 | tf_op jit(solution)/shard_map/all_to_all | solution.py:22
  76.4 0.1 slice_bitcast_fusion.5
  76.5 0.1 slice_bitcast_fusion.7
  76.6 0.1 maximum_bitcast_fusion.1
  76.8 0.1 broadcast_in_dim.36
  76.9 0.1 broadcast_in_dim.34
  77.0 0.2 pad_maximum_fusion
  77.2 35.3 %all_to_all.21 = bf16[64,13,8,128]{3,2,1,0:T(8,128)(2,1)S(1)} all-to-all(bf16[64,13,8,128]{3,2,1,0:T(8,128)(2,1)S(1)} %bitcast.95), channel_id=1, replica_groups=mesh['xh'=2,'zq'=8,'zp'=2,'xl'=2,'y'=4,'core'=2] {'xh','zp','xl','y','co..., dimensions={0} | all-to-all | bytes 3407872 | tf_op jit(solution)/shard_map/all_to_all | solution.py:22
  112.6 0.3 copy.22
  112.9 0.1 slice_bitcast_fusion.panel_ref
  113.0 2.2 %shard_map.50 = (f32[448,896]{1,0:T(8,128)}, f32[256,512]{1,0:T(8,128)}) custom-call(bf16[512,512]{1,0:T(8,128)(2,1)S(1)} %slice_bitcast_fusion.1.rows_ref, bf16[512,896]{1,0:T(8,128)(2,1)S(1)} %slice_bitcast_fusion.panel_ref, bf16[512,256]{1,0:T(8,128)(2,1)S(1)} %bitcast.94, bf16[512,512]{1,0:T(8,128)(2,1)S(1)} %bitcast.93), custom_call_target="tpu_custom_call" | custom-call | tf_op jit(solution)/shard_map/pallas_call | solution.py:51
  (17 shorter events, 0.4 us)
Async XLA Ops:
  0.6 1.0 copy-start
  0.6 34.3 %copy-start.1 = (bf16[512,448]{0,1:T(8,128)(2,1)S(1)}, bf16[512,448]{0,1:T(8,128)(2,1)}, u32[]{:S(2)}) copy-start(bf16[512,448]{0,1:T(8,128)(2,1)} %param.4) | copy-start | bytes 1376260
  2.5 32.3 %all-to-all-start = ((bf16[16,9,8,128]{3,2,1,0:T(8,128)(2,1)}), bf16[16,9,8,128]{3,2,1,0:T(8,128)(2,1)S(1)}, u32[]{:S(2)}, u32[]{:S(2)}) async-start(bf16[16,9,8,128]{3,2,1,0:T(8,128)(2,1)} %fusion.4), calls=%async_computation | async-start | bytes 589824 | tf_op jit(solution)/shard_map/all_to_all | solution.py:22
  18.3 16.6 %collective-permute-start.2 = (bf16[448,512]{1,0:T(8,128)(2,1)}, bf16[448,512]{1,0:T(8,128)(2,1)S(1)}, u32[]{:S(2)}, u32[]{:S(2)}) collective-permute-start(bf16[448,512]{1,0:T(8,128)(2,1)} %bitcast.111), channel_id=1, source_target_pairs={{0,256},{256,0},{1,257},{257,1},{2,258},{258,2},{3,259},{259,3},{4... | collective-permute-start | bytes 1376264 | tf_op jit(solution)/shard_map/ppermute | solution.py:113
  23.7 11.1 %collective-permute-start = (bf16[16,448]{1,0:T(8,128)(2,1)S(1)}, bf16[16,448]{1,0:T(8,128)(2,1)S(1)}, u32[]{:S(2)}, u32[]{:S(2)}) collective-permute-start(bf16[16,448]{1,0:T(8,128)(2,1)S(1)} %get-tuple-element.22), channel_id=1, source_target_pairs={{0,0},{1,2},{2,4},{3,6},{4,8},{5,10},{6,12},{7,14},{8,256},{9,258}... | collective-permute-start | bytes 43016 | tf_op jit(solution)/shard_map/ppermute | solution.py:116
  28.0 6.8 %collective-permute-start.1 = (bf16[16,448]{1,0:T(8,128)(2,1)S(1)}, bf16[16,448]{1,0:T(8,128)(2,1)S(1)}, u32[]{:S(2)}, u32[]{:S(2)}) collective-permute-start(bf16[16,448]{1,0:T(8,128)(2,1)S(1)} %get-tuple-element.23), channel_id=1, source_target_pairs={{0,1},{1,3},{2,5},{3,7},{4,9},{5,11},{6,13},{7,15},{8,257},{9,259}... | collective-permute-start | bytes 43016 | tf_op jit(solution)/shard_map/ppermute | solution.py:117
  54.3 22.1 %all-to-all-start.2 = ((bf16[16,7,8,128]{3,2,1,0:T(8,128)(2,1)}), bf16[16,7,8,128]{3,2,1,0:T(8,128)(2,1)S(1)}, u32[]{:S(2)}, u32[]{:S(2)}) async-start(bf16[16,7,8,128]{3,2,1,0:T(8,128)(2,1)} %bitcast.13), calls=%async_computation.2 | async-start | bytes 458752 | tf_op jit(solution)/shard_map/all_to_all | solution.py:22
  63.8 9.7 %collective-permute-start.3 = (bf16[256,512]{1,0:T(8,128)(2,1)S(1)}, bf16[256,512]{1,0:T(8,128)(2,1)S(1)}, u32[]{:S(2)}, u32[]{:S(2)}) collective-permute-start(bf16[256,512]{1,0:T(8,128)(2,1)S(1)} %bitcast.101), channel_id=1, source_target_pairs={{0,256},{256,0},{1,257},{257,1},{2,258},{258,2},{3,259},{259,3},{4... | collective-permute-start | bytes 786440 | tf_op jit(solution)/shard_map/ppermute | solution.py:136

commit v6 on v5

--- a/solution.py
+++ b/solution.py
@@ -31,32 +31,40 @@
     return lax.dot_general(a, b, CONTRACT, preferred_element_type=jnp.float32)
 
 
-def covariance_kernel(scale, rows_ref, panel_ref, act_rows_ref, cols_ref, grad_ref, act_ref, rows_t, act_t):
-    step = pl.program_id(0)
-
-    @pl.when(step == 0)
-    def _():
-        rows_t[...] = rows_ref[...].T
-        act_t[...] = act_rows_ref[...].T
-
-    for left, right, out in ((rows_t, panel_ref, grad_ref), (act_t, cols_ref, act_ref)):
-        count = out.shape[0]
-        mine = left[pl.ds(pl.multiple_of(step * count, count), count), :]
-        out[...] = jnp.dot(mine, right[...], preferred_element_type=jnp.float32) * scale
+def covariance_kernel(scale, rows_ref, panel_ref, act_rows_ref, cols_ref, grad_ref, act_ref, grad, act, act_t, sems):
+    nx, halves, count, width = act_rows_ref.shape
+    for x in range(nx):
+        for h in range(halves):
+            act_t[h * width : (h + 1) * width, x * count : (x + 1) * count] = act_rows_ref[x, h].T
+    act[...] = jnp.dot(act_t[...], cols_ref[...], preferred_element_type=jnp.float32) * scale
+    copies = [pltpu.make_async_copy(act, act_ref, sems.at[0])]
+    copies[0].start()
+    steps, height, _ = grad.shape
+    rows_t = rows_ref[...].T
+    for k in range(steps):
+        mine = rows_t[k * height : (k + 1) * height]
+        grad[k] = jnp.dot(mine, panel_ref[...], preferred_element_type=jnp.float32) * scale
+        copy = pltpu.make_async_copy(grad.at[k], grad_ref.at[pl.ds(k * height, height)], sems.at[1 + k])
+        copy.start()
+        copies.append(copy)
+    for copy in copies:
+        copy.wait()
 
 
 def covariances(rows, panel, act_rows, cols, height, scale):
     steps = 2
-    outs = [(height, panel.shape[1]), (act_rows.shape[1], cols.shape[1])]
+    grad_shape = (height, panel.shape[1])
+    act_shape = (act_rows.shape[1] * act_rows.shape[3], cols.shape[1])
     return pl.pallas_call(
         functools.partial(covariance_kernel, scale),
-        grid=(steps,),
         in_specs=[pl.BlockSpec(memory_space=pltpu.VMEM)] * 4,
-        out_specs=[pl.BlockSpec((m // steps, n), lambda i: (i, 0)) for m, n in outs],
-        out_shape=[jax.ShapeDtypeStruct(shape, jnp.float32) for shape in outs],
+        out_specs=[pl.BlockSpec(memory_space=pl.ANY)] * 2,
+        out_shape=[jax.ShapeDtypeStruct(shape, jnp.float32) for shape in (grad_shape, act_shape)],
         scratch_shapes=[
-            pltpu.VMEM(rows.shape[::-1], rows.dtype),
-            pltpu.VMEM(act_rows.shape[::-1], act_rows.dtype),
+            pltpu.VMEM((steps, height // steps, grad_shape[1]), jnp.float32),
+            pltpu.VMEM(act_shape, jnp.float32),
+            pltpu.VMEM((act_shape[0], cols.shape[0]), act_rows.dtype),
+            pltpu.SemaphoreType.DMA((1 + steps,)),
         ],
         compiler_params=pltpu.CompilerParams(vmem_limit_bytes=16 * 1024 * 1024),
     )(rows, panel, act_rows, cols)
@@ -98,16 +106,8 @@
     token_count = tok * nx * nz
 
     own_cols = lax.dynamic_slice_in_dim(tokens, col * fcol, fcol, 1)
-    own_token = lax.dynamic_slice_in_dim(tokens, col, 1, 0).reshape(nx, nq, npar, 2, rfeat // 2)
-    own_token = own_token.transpose(1, 3, 0, 2, 4).reshape(nz, 1, nx * npar, rfeat // 2)
-    own_token = jnp.pad(own_token, ((0, 0), (0, 0), (0, 8 - own_token.shape[2]), (0, 0)))
-    sent = to_tiles(own_cols)
-    n_cols = sent.shape[0]
-    sent = jnp.concatenate([jnp.broadcast_to(sent[None], (nz, n_cols, 8, 128)), own_token], axis=1)
-    gathered = exchange(sent, LINE)
-    half = from_tiles(gathered[:, :n_cols], tok).reshape(nz * tok, fcol)
-    picked = gathered[:, n_cols, : nx * npar].reshape(nz // 8, 8, nx, npar, rfeat // 2)
-    picked = picked.transpose(2, 3, 0, 1, 4)
+    half = exchange(jnp.broadcast_to(own_cols[None], (nz, tok, fcol)), LINE)
+    half = half.reshape(nz * tok, fcol)
     swap = [(0, 1), (1, 0)]
     own_weight = weight.T
     other_weight = lax.ppermute(own_weight, "xh", swap)
@@ -130,13 +130,20 @@
     pair = jnp.concatenate([jnp.where(xh == 0, own, other), jnp.where(xh == 0, other, own)], axis=1)
 
     few = tok // npar
+    own_token = lax.dynamic_slice_in_dim(tokens, col, 1, 0).reshape(nx, nq, npar, 2, rfeat // 2)
+    own_token = own_token.transpose(1, 3, 0, 2, 4).reshape(nz, 1, nx * npar, rfeat // 2)
+    own_token = jnp.pad(own_token, ((0, 0), (0, 0), (0, 8 - own_token.shape[2]), (0, 0)))
     pair = to_tiles(pair.reshape(npar, few, 2 * hid))
-    sent = jnp.broadcast_to(pair[None], (nq, *pair.shape)).reshape(nz, -1, 8, 128)
-    lines = exchange(sent, LINE)
+    n_pair = pair.shape[1]
+    sent = jnp.broadcast_to(pair[None], (nq, *pair.shape)).reshape(nz, n_pair, 8, 128)
+    gathered = exchange(jnp.concatenate([sent, own_token], axis=1), LINE)
+    lines = gathered[:, :n_pair]
+    picked = gathered[:, n_pair, : nx * npar].reshape(nz // 8, 8, nx, npar, rfeat // 2)
+    picked = picked.transpose(2, 3, 0, 1, 4)
     other_half = lax.ppermute(half, "xh", swap)
     cols = jnp.stack([jnp.where(xh == 0, half, other_half), jnp.where(xh == 0, other_half, half)])
     cols = cols.reshape(nx, nz, tok, fcol).transpose(0, 2, 1, 3).reshape(-1, fcol)
-    lines, cols = lax.optimization_barrier((lines, cols))
+    lines, picked, cols = lax.optimization_barrier((lines, picked, cols))
     blocks = from_tiles(lines, few).reshape(nq, npar, few, 2 * hid)
 
     panels = jnp.stack(
@@ -163,8 +170,7 @@
 
     panel = from_tiles(pieces[:, :n_panel], few).reshape(-1, 2 * hid)
     row_block = from_tiles(pieces[:, n_panel : n_panel + n_row], few).reshape(-1, LANES)
-    act_rows = pieces[:, n_panel + n_row :].reshape(nx, npar, ncol, nz, rfeat // 2)
-    act_rows = act_rows.transpose(0, 2, 3, 1, 4).reshape(-1, rfeat)
+    act_rows = pieces[:, n_panel + n_row :].reshape(nx, npar, ncol * nz, rfeat // 2)
     grad_cov, act_cov = covariances(row_block, panel, act_rows, cols, hid, 1.0 / token_count)
     return act_cov, grad_cov
 

time: 116 us -> 118 us (1.017)
  blocking collectives: 53.2 us -> 36.1 us
  waiting for transfers between devices: 11 us -> 20.1 us
  starting transfers between devices: 42.1 us -> 51.1 us
  matrix products: 0.47 us -> 2.26 us
    all_to_all x2 -> x1, blocking collectives: 53.2 us -> 36.1 us  [exchange(): return lax.all_to_all(parts, axis, split_axis=0, concat_axis=0, tiled=True)]
    all_to_all x2 -> x3, waiting for transfers between devices: 2.45 us -> 11.6 us  [exchange(): return lax.all_to_all(parts, axis, split_axis=0, concat_axis=0, tiled=True)]
    all_to_all x2 -> x3, starting transfers between devices: 25.2 us -> 34.3 us  [exchange(): return lax.all_to_all(parts, axis, split_axis=0, concat_axis=0, tiled=True)]
    dot_general x1, matrix products: 0.47 us -> 2.26 us  [shards(): lax.dot_general(half, both, (((1,), (1,)), ((), ())), preferred_element_t...]
  transfers between devices with their start and end apart: 6 -> 7, of which waited for: 3 -> 4; matrix products, arithmetic and copies ran while one was open for 1% -> 1% of each run, Pallas kernels for 0% -> 0%
where the time goes in v6:
time: 118 us; the launch traced here: 117 us
  starting transfers between devices  51.1 us (43%)
  blocking collectives  36.1 us (31%)
  waiting for transfers between devices  20.1 us (17%)
  local copies, waits for them, and re-layouts  2.72 us (2%)
  other arithmetic  2.27 us (2%)
  matrix products  2.26 us (2%)
  Pallas kernels  1.76 us (1%)
    all_to_all x1, blocking collectives, exchange(): return lax.all_to_all(parts, axis, split_axis=0, concat_axis=0, tiled=True)  36.1 us
    all_to_all x3, starting transfers between devices, exchange(): return lax.all_to_all(parts, axis, split_axis=0, concat_axis=0, tiled=True)  34.3 us
    all_to_all x3, waiting for transfers between devices, exchange(): return lax.all_to_all(parts, axis, split_axis=0, concat_axis=0, tiled=True)  11.6 us
    ppermute x1, waiting for transfers between devices, shards(): other_half = lax.ppermute(half, 'xh', swap)  5.74 us
    ppermute x1, starting transfers between devices, shards(): other_weight = lax.ppermute(own_weight, 'xh', swap)  4.65 us
    ppermute x1, starting transfers between devices, shards(): lax.ppermute(jnp.where(xh == 0, halves[0], halves[1]), LEVEL, moves(0))  4.31 us
    ppermute x1, starting transfers between devices, shards(): other_half = lax.ppermute(half, 'xh', swap)  4 us
    ppermute x1, starting transfers between devices, shards(): lax.ppermute(jnp.where(xh == 0, halves[1], halves[0]), LEVEL, moves(1))  3.92 us
  transfers between devices with their start and end apart: 7, of which 4 were waited for; matrix products, arithmetic and copies ran while one was open for 1% of the time, Pallas kernels for 0%

profile of v6, /device:TPU:1, one launch (start us, length us, event | category | flops | bytes accessed | tf_op | source)
XLA Modules:
  0.0 117.3 jit_solution(14801509165700110672)
XLA Ops:
  0.6 0.0 copy-start
  0.7 0.9 copy-done
  1.6 0.7 broadcast_in_dim.14
  2.3 15.7 %all-to-all-start = ((bf16[16,16,512]{2,1,0:T(8,128)(2,1)}), bf16[16,16,512]{2,1,0:T(8,128)(2,1)S(1)}, u32[]{:S(2)}, u32[]{:S(2)}) async-start(bf16[16,16,512]{2,1,0:T(8,128)(2,1)} %broadcast_in_dim.14), calls=%async_computation | async-start | bytes 524288 | tf_op jit(solution)/shard_map/all_to_all | solution.py:22
  18.1 4.7 %collective-permute-start.2 = (bf16[448,512]{1,0:T(8,128)(2,1)}, bf16[448,512]{1,0:T(8,128)(2,1)S(1)}, u32[]{:S(2)}, u32[]{:S(2)}) collective-permute-start(bf16[448,512]{1,0:T(8,128)(2,1)} %bitcast.92), channel_id=1, source_target_pairs={{0,256},{256,0},{1,257},{257,1},{2,258},{258,2},{3,259},{259,3},{4... | collective-permute-start | bytes 1376264 | tf_op jit(solution)/shard_map/ppermute | solution.py:113
  22.7 0.7 broadcast_select_fusion.7
  23.5 4.3 %collective-permute-start = (bf16[16,448]{1,0:T(8,128)(2,1)S(1)}, bf16[16,448]{1,0:T(8,128)(2,1)S(1)}, u32[]{:S(2)}, u32[]{:S(2)}) collective-permute-start(bf16[16,448]{1,0:T(8,128)(2,1)S(1)} %get-tuple-element.24), channel_id=1, source_target_pairs={{0,0},{1,2},{2,4},{3,6},{4,8},{5,10},{6,12},{7,14},{8,256},{9,258}... | collective-permute-start | bytes 43016 | tf_op jit(solution)/shard_map/ppermute | solution.py:116
  27.8 3.9 %collective-permute-start.1 = (bf16[16,448]{1,0:T(8,128)(2,1)S(1)}, bf16[16,448]{1,0:T(8,128)(2,1)S(1)}, u32[]{:S(2)}, u32[]{:S(2)}) collective-permute-start(bf16[16,448]{1,0:T(8,128)(2,1)S(1)} %get-tuple-element.25), channel_id=1, source_target_pairs={{0,1},{1,3},{2,5},{3,7},{4,9},{5,11},{6,13},{7,15},{8,257},{9,259}... | collective-permute-start | bytes 43016 | tf_op jit(solution)/shard_map/ppermute | solution.py:117
  31.7 2.8 %collective-permute-done = bf16[16,448]{1,0:T(8,128)(2,1)S(1)} collective-permute-done((bf16[16,448]{1,0:T(8,128)(2,1)S(1)}, bf16[16,448]{1,0:T(8,128)(2,1)S(1)}, u32[]{:S(2)}, u32[]{:S(2)}) %collective-permute-start) | collective-permute-done | bytes 14368 | tf_op jit(solution)/shard_map/ppermute | solution.py:116
  34.6 0.0 collective-permute-done.1
  34.6 0.1 pad_maximum_fusion.2
  34.7 0.0 all-to-all-done
  34.7 0.0 collective-permute-done.2
  34.7 2.3 %convolution_convert_fusion = bf16[256,896]{1,0:T(8,128)(2,1)} fusion(bf16[256,512]{1,0:T(8,128)(2,1)S(1)} %bitcast.82, bf16[448,512]{1,0:T(8,128)(2,1)S(1)} %collective-permute-done.2, bf16[448,512]{1,0:T(8,128)(2,1)} %bitcast.93), kind=kOutput, calls=%fused_computation.1 | convolution fusion | flops 236945408 | bytes 1638400 | tf_op jit(solution)/shard_map/dot_general | solution.py:125
  36.9 8.1 %all-to-all-start.1 = ((bf16[16,16,896]{2,1,0:T(8,128)(2,1)}), bf16[16,16,896]{2,1,0:T(8,128)(2,1)S(1)}, u32[]{:S(2)}, u32[]{:S(2)}) async-start(bf16[16,16,896]{2,1,0:T(8,128)(2,1)} %bitcast.2), calls=%async_computation.1 | async-start | bytes 917504 | tf_op jit(solution)/shard_map/all_to_all | solution.py:22
  45.1 0.1 dynamic-slice_reduce_fusion
  45.2 8.9 %all-to-all-done.1 = bf16[16,16,896]{2,1,0:T(8,128)(2,1)S(1)} async-done(((bf16[16,16,896]{2,1,0:T(8,128)(2,1)}), bf16[16,16,896]{2,1,0:T(8,128)(2,1)S(1)}, u32[]{:S(2)}, u32[]{:S(2)}) %all-to-all-start.1) | async-done | bytes 458784 | tf_op jit(solution)/shard_map/all_to_all | solution.py:22
  54.2 0.1 convert_reduce_fusion
  54.3 0.1 broadcast_select_fusion.5
  54.3 0.1 maximum_bitcast_fusion.3
  54.5 0.7 fusion.4
  55.2 10.4 %all-to-all-start.2 = ((bf16[16,8,8,128]{3,2,1,0:T(8,128)(2,1)}), bf16[16,8,8,128]{3,2,1,0:T(8,128)(2,1)S(1)}, u32[]{:S(2)}, u32[]{:S(2)}) async-start(bf16[16,8,8,128]{3,2,1,0:T(8,128)(2,1)} %fusion.4), calls=%async_computation.2 | async-start | bytes 524288 | tf_op jit(solution)/shard_map/all_to_all | solution.py:22
  65.6 4.0 %collective-permute-start.3 = (bf16[256,512]{1,0:T(8,128)(2,1)S(1)}, bf16[256,512]{1,0:T(8,128)(2,1)S(1)}, u32[]{:S(2)}, u32[]{:S(2)}) collective-permute-start(bf16[256,512]{1,0:T(8,128)(2,1)S(1)} %bitcast.83), channel_id=1, source_target_pairs={{0,256},{256,0},{1,257},{257,1},{2,258},{258,2},{3,259},{259,3},{4... | collective-permute-start | bytes 786440 | tf_op jit(solution)/shard_map/ppermute | solution.py:143
  69.6 5.7 %collective-permute-done.3 = bf16[256,512]{1,0:T(8,128)(2,1)S(1)} collective-permute-done((bf16[256,512]{1,0:T(8,128)(2,1)S(1)}, bf16[256,512]{1,0:T(8,128)(2,1)S(1)}, u32[]{:S(2)}, u32[]{:S(2)}) %collective-permute-start.3) | collective-permute-done | bytes 262176 | tf_op jit(solution)/shard_map/ppermute | solution.py:143
  75.4 0.1 maximum_bitcast_fusion
  75.4 0.3 copy.17
  75.7 2.6 %all-to-all-done.2 = bf16[16,8,8,128]{3,2,1,0:T(8,128)(2,1)S(1)} async-done(((bf16[16,8,8,128]{3,2,1,0:T(8,128)(2,1)}), bf16[16,8,8,128]{3,2,1,0:T(8,128)(2,1)S(1)}, u32[]{:S(2)}, u32[]{:S(2)}) %all-to-all-start.2) | async-done | bytes 262176 | tf_op jit(solution)/shard_map/all_to_all | solution.py:22
  78.4 0.1 slice_bitcast_fusion.5
  78.6 0.1 slice_bitcast_fusion.7
  78.7 0.1 maximum_bitcast_fusion.1
  78.8 0.1 broadcast_in_dim.34
  78.9 0.1 broadcast_in_dim.32
  79.0 0.2 pad_maximum_fusion
  79.3 36.1 %all_to_all.20 = bf16[64,13,8,128]{3,2,1,0:T(8,128)(2,1)S(1)} all-to-all(bf16[64,13,8,128]{3,2,1,0:T(8,128)(2,1)S(1)} %bitcast.79), channel_id=1, replica_groups=mesh['xh'=2,'zq'=8,'zp'=2,'xl'=2,'y'=4,'core'=2] {'xh','zp','xl','y','co..., dimensions={0} | all-to-all | bytes 3407872 | tf_op jit(solution)/shard_map/all_to_all | solution.py:22
  115.4 0.1 slice_bitcast_fusion.panel_ref
  115.5 1.8 %shard_map.50 = (f32[448,896]{1,0:T(8,128)}, f32[256,512]{1,0:T(8,128)}) custom-call(bf16[512,512]{1,0:T(8,128)(2,1)S(1)} %slice_bitcast_fusion.1.rows_ref, bf16[512,896]{1,0:T(8,128)(2,1)S(1)} %slice_bitcast_fusion.panel_ref, bf16[2,2,256,128]{3,2,1,0:T(8,128)(2,1)S(1)} %bitcast.78, bf16[512,512]{1,0:T(8,128)(2,1)S(1)} %bitcast.77), custom_call_target="tpu_custom_call" | custom-call | tf_op jit(solution)/shard_map/pallas_call | solution.py:58
  (16 shorter events, 0.3 us)
Async XLA Ops:
  0.6 1.0 copy-start
  2.3 32.3 %all-to-all-start = ((bf16[16,16,512]{2,1,0:T(8,128)(2,1)}), bf16[16,16,512]{2,1,0:T(8,128)(2,1)S(1)}, u32[]{:S(2)}, u32[]{:S(2)}) async-start(bf16[16,16,512]{2,1,0:T(8,128)(2,1)} %broadcast_in_dim.14), calls=%async_computation | async-start | bytes 524288 | tf_op jit(solution)/shard_map/all_to_all | solution.py:22
  18.1 16.6 %collective-permute-start.2 = (bf16[448,512]{1,0:T(8,128)(2,1)}, bf16[448,512]{1,0:T(8,128)(2,1)S(1)}, u32[]{:S(2)}, u32[]{:S(2)}) collective-permute-start(bf16[448,512]{1,0:T(8,128)(2,1)} %bitcast.92), channel_id=1, source_target_pairs={{0,256},{256,0},{1,257},{257,1},{2,258},{258,2},{3,259},{259,3},{4... | collective-permute-start | bytes 1376264 | tf_op jit(solution)/shard_map/ppermute | solution.py:113
  23.5 11.1 %collective-permute-start = (bf16[16,448]{1,0:T(8,128)(2,1)S(1)}, bf16[16,448]{1,0:T(8,128)(2,1)S(1)}, u32[]{:S(2)}, u32[]{:S(2)}) collective-permute-start(bf16[16,448]{1,0:T(8,128)(2,1)S(1)} %get-tuple-element.24), channel_id=1, source_target_pairs={{0,0},{1,2},{2,4},{3,6},{4,8},{5,10},{6,12},{7,14},{8,256},{9,258}... | collective-permute-start | bytes 43016 | tf_op jit(solution)/shard_map/ppermute | solution.py:116
  27.8 6.8 %collective-permute-start.1 = (bf16[16,448]{1,0:T(8,128)(2,1)S(1)}, bf16[16,448]{1,0:T(8,128)(2,1)S(1)}, u32[]{:S(2)}, u32[]{:S(2)}) collective-permute-start(bf16[16,448]{1,0:T(8,128)(2,1)S(1)} %get-tuple-element.25), channel_id=1, source_target_pairs={{0,1},{1,3},{2,5},{3,7},{4,9},{5,11},{6,13},{7,15},{8,257},{9,259}... | collective-permute-start | bytes 43016 | tf_op jit(solution)/shard_map/ppermute | solution.py:117
  36.9 17.2 %all-to-all-start.1 = ((bf16[16,16,896]{2,1,0:T(8,128)(2,1)}), bf16[16,16,896]{2,1,0:T(8,128)(2,1)S(1)}, u32[]{:S(2)}, u32[]{:S(2)}) async-start(bf16[16,16,896]{2,1,0:T(8,128)(2,1)} %bitcast.2), calls=%async_computation.1 | async-start | bytes 917504 | tf_op jit(solution)/shard_map/all_to_all | solution.py:22
  55.2 23.2 %all-to-all-start.2 = ((bf16[16,8,8,128]{3,2,1,0:T(8,128)(2,1)}), bf16[16,8,8,128]{3,2,1,0:T(8,128)(2,1)S(1)}, u32[]{:S(2)}, u32[]{:S(2)}) async-start(bf16[16,8,8,128]{3,2,1,0:T(8,128)(2,1)} %fusion.4), calls=%async_computation.2 | async-start | bytes 524288 | tf_op jit(solution)/shard_map/all_to_all | solution.py:22
  65.6 9.7 %collective-permute-start.3 = (bf16[256,512]{1,0:T(8,128)(2,1)S(1)}, bf16[256,512]{1,0:T(8,128)(2,1)S(1)}, u32[]{:S(2)}, u32[]{:S(2)}) collective-permute-start(bf16[256,512]{1,0:T(8,128)(2,1)S(1)} %bitcast.83), channel_id=1, source_target_pairs={{0,256},{256,0},{1,257},{257,1},{2,258},{258,2},{3,259},{259,3},{4... | collective-permute-start | bytes 786440 | tf_op jit(solution)/shard_map/ppermute | solution.py:143

commit v7 on v6

--- a/solution.py
+++ b/solution.py
@@ -106,8 +106,16 @@
     token_count = tok * nx * nz
 
     own_cols = lax.dynamic_slice_in_dim(tokens, col * fcol, fcol, 1)
-    half = exchange(jnp.broadcast_to(own_cols[None], (nz, tok, fcol)), LINE)
-    half = half.reshape(nz * tok, fcol)
+    own_token = lax.dynamic_slice_in_dim(tokens, col, 1, 0).reshape(nx, nq, npar, 2, rfeat // 2)
+    own_token = own_token.transpose(1, 3, 0, 2, 4).reshape(nz, 1, nx * npar, rfeat // 2)
+    own_token = jnp.pad(own_token, ((0, 0), (0, 0), (0, 8 - own_token.shape[2]), (0, 0)))
+    sent = to_tiles(own_cols)
+    n_cols = sent.shape[0]
+    sent = jnp.concatenate([jnp.broadcast_to(sent[None], (nz, n_cols, 8, 128)), own_token], axis=1)
+    gathered = exchange(sent, LINE)
+    half = from_tiles(gathered[:, :n_cols], tok).reshape(nz * tok, fcol)
+    picked = gathered[:, n_cols, : nx * npar].reshape(nz // 8, 8, nx, npar, rfeat // 2)
+    picked = picked.transpose(2, 3, 0, 1, 4)
     swap = [(0, 1), (1, 0)]
     own_weight = weight.T
     other_weight = lax.ppermute(own_weight, "xh", swap)
@@ -130,20 +138,13 @@
     pair = jnp.concatenate([jnp.where(xh == 0, own, other), jnp.where(xh == 0, other, own)], axis=1)
 
     few = tok // npar
-    own_token = lax.dynamic_slice_in_dim(tokens, col, 1, 0).reshape(nx, nq, npar, 2, rfeat // 2)
-    own_token = own_token.transpose(1, 3, 0, 2, 4).reshape(nz, 1, nx * npar, rfeat // 2)
-    own_token = jnp.pad(own_token, ((0, 0), (0, 0), (0, 8 - own_token.shape[2]), (0, 0)))
     pair = to_tiles(pair.reshape(npar, few, 2 * hid))
-    n_pair = pair.shape[1]
-    sent = jnp.broadcast_to(pair[None], (nq, *pair.shape)).reshape(nz, n_pair, 8, 128)
-    gathered = exchange(jnp.concatenate([sent, own_token], axis=1), LINE)
-    lines = gathered[:, :n_pair]
-    picked = gathered[:, n_pair, : nx * npar].reshape(nz // 8, 8, nx, npar, rfeat // 2)
-    picked = picked.transpose(2, 3, 0, 1, 4)
+    sent = jnp.broadcast_to(pair[None], (nq, *pair.shape)).reshape(nz, -1, 8, 128)
+    lines = exchange(sent, LINE)
     other_half = lax.ppermute(half, "xh", swap)
     cols = jnp.stack([jnp.where(xh == 0, half, other_half), jnp.where(xh == 0, other_half, half)])
     cols = cols.reshape(nx, nz, tok, fcol).transpose(0, 2, 1, 3).reshape(-1, fcol)
-    lines, picked, cols = lax.optimization_barrier((lines, picked, cols))
+    lines, cols = lax.optimization_barrier((lines, cols))
     blocks = from_tiles(lines, few).reshape(nq, npar, few, 2 * hid)
 
     panels = jnp.stack(

time: 118 us -> 115 us (0.975)
  blocking collectives: 36.1 us -> 53.2 us
  waiting for transfers between devices: 20.1 us -> 11 us
  starting transfers between devices: 51.1 us -> 42.1 us
  matrix products: 2.26 us -> 0.47 us
    all_to_all x1 -> x2, blocking collectives: 36.1 us -> 53.2 us  [exchange(): return lax.all_to_all(parts, axis, split_axis=0, concat_axis=0, tiled=True)]
    all_to_all x3 -> x2, waiting for transfers between devices: 11.6 us -> 2.45 us  [exchange(): return lax.all_to_all(parts, axis, split_axis=0, concat_axis=0, tiled=True)]
    all_to_all x3 -> x2, starting transfers between devices: 34.3 us -> 25.2 us  [exchange(): return lax.all_to_all(parts, axis, split_axis=0, concat_axis=0, tiled=True)]
    dot_general x1, matrix products: 2.26 us -> 0.47 us  [shards(): lax.dot_general(half, both, (((1,), (1,)), ((), ())), preferred_element_t...]
  transfers between devices with their start and end apart: 7 -> 6, of which waited for: 4 -> 3; matrix products, arithmetic and copies ran while one was open for 1% -> 1% of each run, Pallas kernels for 0% -> 0%
where the time goes in v7:
time: 115 us; the launch traced here: 114 us
  blocking collectives  53.2 us (46%)
  starting transfers between devices  42.1 us (37%)
  waiting for transfers between devices  11 us (10%)
  local copies, waits for them, and re-layouts  2.72 us (2%)
  other arithmetic  2.27 us (2%)
  Pallas kernels  1.76 us (2%)
    all_to_all x2, blocking collectives, exchange(): return lax.all_to_all(parts, axis, split_axis=0, concat_axis=0, tiled=True)  53.2 us
    all_to_all x2, starting transfers between devices, exchange(): return lax.all_to_all(parts, axis, split_axis=0, concat_axis=0, tiled=True)  25.2 us
    ppermute x1, waiting for transfers between devices, shards(): other_half = lax.ppermute(half, 'xh', swap)  5.72 us
    ppermute x1, starting transfers between devices, shards(): other_weight = lax.ppermute(own_weight, 'xh', swap)  4.65 us
    ppermute x1, starting transfers between devices, shards(): lax.ppermute(jnp.where(xh == 0, halves[0], halves[1]), LEVEL, moves(0))  4.31 us
    ppermute x1, starting transfers between devices, shards(): other_half = lax.ppermute(half, 'xh', swap)  3.99 us
    ppermute x1, starting transfers between devices, shards(): lax.ppermute(jnp.where(xh == 0, halves[1], halves[0]), LEVEL, moves(1))  3.92 us
    ppermute x1, waiting for transfers between devices, shards(): lax.ppermute(jnp.where(xh == 0, halves[0], halves[1]), LEVEL, moves(0))  2.83 us
  transfers between devices with their start and end apart: 6, of which 3 were waited for; matrix products, arithmetic and copies ran while one was open for 1% of the time, Pallas kernels for 0%

profile of v7, /device:TPU:1, one launch (start us, length us, event | category | flops | bytes accessed | tf_op | source)
XLA Modules:
  0.0 114.4 jit_solution(13320850060723734462)
XLA Ops:
  0.6 0.0 copy-start
  0.6 0.0 copy-start.1
  0.7 0.9 copy-done
  1.6 0.1 dynamic-slice_reduce_fusion
  1.8 0.7 fusion.4
  2.5 15.7 %all-to-all-start = ((bf16[16,9,8,128]{3,2,1,0:T(8,128)(2,1)}), bf16[16,9,8,128]{3,2,1,0:T(8,128)(2,1)S(1)}, u32[]{:S(2)}, u32[]{:S(2)}) async-start(bf16[16,9,8,128]{3,2,1,0:T(8,128)(2,1)} %fusion.4), calls=%async_computation | async-start | bytes 589824 | tf_op jit(solution)/shard_map/all_to_all | solution.py:22
  18.3 4.7 %collective-permute-start.2 = (bf16[448,512]{1,0:T(8,128)(2,1)}, bf16[448,512]{1,0:T(8,128)(2,1)S(1)}, u32[]{:S(2)}, u32[]{:S(2)}) collective-permute-start(bf16[448,512]{1,0:T(8,128)(2,1)} %bitcast.102), channel_id=1, source_target_pairs={{0,256},{256,0},{1,257},{257,1},{2,258},{258,2},{3,259},{259,3},{4... | collective-permute-start | bytes 1376264 | tf_op jit(solution)/shard_map/ppermute | solution.py:121
  23.0 0.7 broadcast_select_fusion.7
  23.7 4.3 %collective-permute-start = (bf16[16,448]{1,0:T(8,128)(2,1)S(1)}, bf16[16,448]{1,0:T(8,128)(2,1)S(1)}, u32[]{:S(2)}, u32[]{:S(2)}) collective-permute-start(bf16[16,448]{1,0:T(8,128)(2,1)S(1)} %get-tuple-element.22), channel_id=1, source_target_pairs={{0,0},{1,2},{2,4},{3,6},{4,8},{5,10},{6,12},{7,14},{8,256},{9,258}... | collective-permute-start | bytes 43016 | tf_op jit(solution)/shard_map/ppermute | solution.py:124
  28.0 3.9 %collective-permute-start.1 = (bf16[16,448]{1,0:T(8,128)(2,1)S(1)}, bf16[16,448]{1,0:T(8,128)(2,1)S(1)}, u32[]{:S(2)}, u32[]{:S(2)}) collective-permute-start(bf16[16,448]{1,0:T(8,128)(2,1)S(1)} %get-tuple-element.23), channel_id=1, source_target_pairs={{0,1},{1,3},{2,5},{3,7},{4,9},{5,11},{6,13},{7,15},{8,257},{9,259}... | collective-permute-start | bytes 43016 | tf_op jit(solution)/shard_map/ppermute | solution.py:125
  32.0 2.8 %collective-permute-done = bf16[16,448]{1,0:T(8,128)(2,1)S(1)} collective-permute-done((bf16[16,448]{1,0:T(8,128)(2,1)S(1)}, bf16[16,448]{1,0:T(8,128)(2,1)S(1)}, u32[]{:S(2)}, u32[]{:S(2)}) %collective-permute-start) | collective-permute-done | bytes 14368 | tf_op jit(solution)/shard_map/ppermute | solution.py:124
  34.8 0.0 collective-permute-done.1
  34.8 0.1 pad_maximum_fusion.2
  34.9 0.0 all-to-all-done
  34.9 0.0 collective-permute-done.2
  34.9 0.0 copy-done.1
  34.9 0.5 convolution_convert_fusion
  35.4 17.9 %all_to_all.20 = bf16[16,16,896]{2,1,0:T(8,128)(2,1)S(1)} all-to-all(bf16[16,16,896]{2,1,0:T(8,128)(2,1)S(1)} %bitcast.97), channel_id=1, replica_groups=mesh['xh'=2,'zq'=8,'zp'=2,'xl'=2,'y'=4,'core'=2] {'xl','y','core'}, dimensions={0} | all-to-all | bytes 917504 | tf_op jit(solution)/shard_map/all_to_all | solution.py:22
  53.3 0.1 convert_reduce_fusion
  53.5 0.1 broadcast_select_fusion.5
  53.5 0.1 maximum_bitcast_fusion.3
  53.6 0.7 broadcast_in_dim.33
  54.3 9.5 %all-to-all-start.2 = ((bf16[16,7,8,128]{3,2,1,0:T(8,128)(2,1)}), bf16[16,7,8,128]{3,2,1,0:T(8,128)(2,1)S(1)}, u32[]{:S(2)}, u32[]{:S(2)}) async-start(bf16[16,7,8,128]{3,2,1,0:T(8,128)(2,1)} %bitcast.13), calls=%async_computation.2 | async-start | bytes 458752 | tf_op jit(solution)/shard_map/all_to_all | solution.py:22
  63.8 4.0 %collective-permute-start.3 = (bf16[256,512]{1,0:T(8,128)(2,1)S(1)}, bf16[256,512]{1,0:T(8,128)(2,1)S(1)}, u32[]{:S(2)}, u32[]{:S(2)}) collective-permute-start(bf16[256,512]{1,0:T(8,128)(2,1)S(1)} %bitcast.92), channel_id=1, source_target_pairs={{0,256},{256,0},{1,257},{257,1},{2,258},{258,2},{3,259},{259,3},{4... | collective-permute-start | bytes 786440 | tf_op jit(solution)/shard_map/ppermute | solution.py:144
  67.8 5.7 %collective-permute-done.3 = bf16[256,512]{1,0:T(8,128)(2,1)S(1)} collective-permute-done((bf16[256,512]{1,0:T(8,128)(2,1)S(1)}, bf16[256,512]{1,0:T(8,128)(2,1)S(1)}, u32[]{:S(2)}, u32[]{:S(2)}) %collective-permute-start.3) | collective-permute-done | bytes 262176 | tf_op jit(solution)/shard_map/ppermute | solution.py:144
  73.6 0.1 maximum_bitcast_fusion
  73.7 0.3 copy.16
  74.0 2.4 %all-to-all-done.2 = bf16[16,7,8,128]{3,2,1,0:T(8,128)(2,1)S(1)} async-done(((bf16[16,7,8,128]{3,2,1,0:T(8,128)(2,1)}), bf16[16,7,8,128]{3,2,1,0:T(8,128)(2,1)S(1)}, u32[]{:S(2)}, u32[]{:S(2)}) %all-to-all-start.2) | async-done | bytes 229408 | tf_op jit(solution)/shard_map/all_to_all | solution.py:22
  76.4 0.1 slice_bitcast_fusion.5
  76.5 0.1 slice_bitcast_fusion.7
  76.6 0.1 maximum_bitcast_fusion.1
  76.8 0.1 broadcast_in_dim.36
  76.9 0.1 broadcast_in_dim.34
  77.0 0.2 pad_maximum_fusion
  77.2 35.3 %all_to_all.21 = bf16[64,13,8,128]{3,2,1,0:T(8,128)(2,1)S(1)} all-to-all(bf16[64,13,8,128]{3,2,1,0:T(8,128)(2,1)S(1)} %bitcast.88), channel_id=1, replica_groups=mesh['xh'=2,'zq'=8,'zp'=2,'xl'=2,'y'=4,'core'=2] {'xh','zp','xl','y','co..., dimensions={0} | all-to-all | bytes 3407872 | tf_op jit(solution)/shard_map/all_to_all | solution.py:22
  112.6 0.1 slice_bitcast_fusion.panel_ref
  112.7 1.8 %shard_map.50 = (f32[448,896]{1,0:T(8,128)}, f32[256,512]{1,0:T(8,128)}) custom-call(bf16[512,512]{1,0:T(8,128)(2,1)S(1)} %slice_bitcast_fusion.1.rows_ref, bf16[512,896]{1,0:T(8,128)(2,1)S(1)} %slice_bitcast_fusion.panel_ref, bf16[2,2,256,128]{3,2,1,0:T(8,128)(2,1)S(1)} %bitcast.87, bf16[512,512]{1,0:T(8,128)(2,1)S(1)} %bitcast.86), custom_call_target="tpu_custom_call" | custom-call | tf_op jit(solution)/shard_map/pallas_call | solution.py:58
  (16 shorter events, 0.3 us)
Async XLA Ops:
  0.6 1.0 copy-start
  0.6 34.3 %copy-start.1 = (bf16[512,448]{0,1:T(8,128)(2,1)S(1)}, bf16[512,448]{0,1:T(8,128)(2,1)}, u32[]{:S(2)}) copy-start(bf16[512,448]{0,1:T(8,128)(2,1)} %param.4) | copy-start | bytes 1376260
  2.5 32.3 %all-to-all-start = ((bf16[16,9,8,128]{3,2,1,0:T(8,128)(2,1)}), bf16[16,9,8,128]{3,2,1,0:T(8,128)(2,1)S(1)}, u32[]{:S(2)}, u32[]{:S(2)}) async-start(bf16[16,9,8,128]{3,2,1,0:T(8,128)(2,1)} %fusion.4), calls=%async_computation | async-start | bytes 589824 | tf_op jit(solution)/shard_map/all_to_all | solution.py:22
  18.3 16.6 %collective-permute-start.2 = (bf16[448,512]{1,0:T(8,128)(2,1)}, bf16[448,512]{1,0:T(8,128)(2,1)S(1)}, u32[]{:S(2)}, u32[]{:S(2)}) collective-permute-start(bf16[448,512]{1,0:T(8,128)(2,1)} %bitcast.102), channel_id=1, source_target_pairs={{0,256},{256,0},{1,257},{257,1},{2,258},{258,2},{3,259},{259,3},{4... | collective-permute-start | bytes 1376264 | tf_op jit(solution)/shard_map/ppermute | solution.py:121
  23.7 11.1 %collective-permute-start = (bf16[16,448]{1,0:T(8,128)(2,1)S(1)}, bf16[16,448]{1,0:T(8,128)(2,1)S(1)}, u32[]{:S(2)}, u32[]{:S(2)}) collective-permute-start(bf16[16,448]{1,0:T(8,128)(2,1)S(1)} %get-tuple-element.22), channel_id=1, source_target_pairs={{0,0},{1,2},{2,4},{3,6},{4,8},{5,10},{6,12},{7,14},{8,256},{9,258}... | collective-permute-start | bytes 43016 | tf_op jit(solution)/shard_map/ppermute | solution.py:124
  28.0 6.8 %collective-permute-start.1 = (bf16[16,448]{1,0:T(8,128)(2,1)S(1)}, bf16[16,448]{1,0:T(8,128)(2,1)S(1)}, u32[]{:S(2)}, u32[]{:S(2)}) collective-permute-start(bf16[16,448]{1,0:T(8,128)(2,1)S(1)} %get-tuple-element.23), channel_id=1, source_target_pairs={{0,1},{1,3},{2,5},{3,7},{4,9},{5,11},{6,13},{7,15},{8,257},{9,259}... | collective-permute-start | bytes 43016 | tf_op jit(solution)/shard_map/ppermute | solution.py:125
  54.3 22.1 %all-to-all-start.2 = ((bf16[16,7,8,128]{3,2,1,0:T(8,128)(2,1)}), bf16[16,7,8,128]{3,2,1,0:T(8,128)(2,1)S(1)}, u32[]{:S(2)}, u32[]{:S(2)}) async-start(bf16[16,7,8,128]{3,2,1,0:T(8,128)(2,1)} %bitcast.13), calls=%async_computation.2 | async-start | bytes 458752 | tf_op jit(solution)/shard_map/all_to_all | solution.py:22
  63.8 9.7 %collective-permute-start.3 = (bf16[256,512]{1,0:T(8,128)(2,1)S(1)}, bf16[256,512]{1,0:T(8,128)(2,1)S(1)}, u32[]{:S(2)}, u32[]{:S(2)}) collective-permute-start(bf16[256,512]{1,0:T(8,128)(2,1)S(1)} %bitcast.92), channel_id=1, source_target_pairs={{0,256},{256,0},{1,257},{257,1},{2,258},{258,2},{3,259},{259,3},{4... | collective-permute-start | bytes 786440 | tf_op jit(solution)/shard_map/ppermute | solution.py:144

commit v8 on v7

--- a/solution.py
+++ b/solution.py
@@ -131,8 +131,8 @@
 
     both = jnp.concatenate([own_weight, other_weight], axis=0)
     part = lax.dot_general(half, both, (((1,), (1,)), ((), ())), preferred_element_type=jnp.float32)
-    part = part.astype(jnp.bfloat16).reshape(ncol, tok, 2 * hid)
-    pre_act = jnp.sum(exchange(part, COL).astype(jnp.float32), axis=0)
+    part = part.reshape(ncol, tok, 2 * hid)
+    pre_act = jnp.sum(exchange(part, COL), axis=0)
     slope = (cot.astype(jnp.float32) * silu_slope(pre_act)).astype(jnp.bfloat16)
     own, other = slope[:, :hid], slope[:, hid:]
     pair = jnp.concatenate([jnp.where(xh == 0, own, other), jnp.where(xh == 0, other, own)], axis=1)

time: 115 us -> 120 us (1.043)
  blocking collectives: 53.2 us -> 58.1 us
    all_to_all x2, blocking collectives: 53.2 us -> 58.1 us  [exchange(): return lax.all_to_all(parts, axis, split_axis=0, concat_axis=0, tiled=True)]
where the time goes in v8:
time: 120 us; the launch traced here: 119 us
  blocking collectives  58.1 us (48%)
  starting transfers between devices  42.1 us (35%)
  waiting for transfers between devices  11 us (9%)
  local copies, waits for them, and re-layouts  2.72 us (2%)
  other arithmetic  2.26 us (2%)
  Pallas kernels  1.76 us (1%)
    all_to_all x2, blocking collectives, exchange(): return lax.all_to_all(parts, axis, split_axis=0, concat_axis=0, tiled=True)  58.1 us
    all_to_all x2, starting transfers between devices, exchange(): return lax.all_to_all(parts, axis, split_axis=0, concat_axis=0, tiled=True)  25.2 us
    ppermute x1, waiting for transfers between devices, shards(): other_half = lax.ppermute(half, 'xh', swap)  5.71 us
    ppermute x1, starting transfers between devices, shards(): other_weight = lax.ppermute(own_weight, 'xh', swap)  4.65 us
    ppermute x1, starting transfers between devices, shards(): lax.ppermute(jnp.where(xh == 0, halves[0], halves[1]), LEVEL, moves(0))  4.31 us
    ppermute x1, starting transfers between devices, shards(): other_half = lax.ppermute(half, 'xh', swap)  3.99 us
    ppermute x1, starting transfers between devices, shards(): lax.ppermute(jnp.where(xh == 0, halves[1], halves[0]), LEVEL, moves(1))  3.92 us
    ppermute x1, waiting for transfers between devices, shards(): lax.ppermute(jnp.where(xh == 0, halves[0], halves[1]), LEVEL, moves(0))  2.83 us
  transfers between devices with their start and end apart: 6, of which 3 were waited for; matrix products, arithmetic and copies ran while one was open for 1% of the time, Pallas kernels for 0%

profile of v8, /device:TPU:1, one launch (start us, length us, event | category | flops | bytes accessed | tf_op | source)
XLA Modules:
  0.0 119.3 jit_solution(186700226816879239)
XLA Ops:
  0.6 0.0 copy-start
  0.6 0.0 copy-start.1
  0.7 0.9 copy-done
  1.6 0.1 dynamic-slice_reduce_fusion
  1.8 0.7 fusion.5
  2.5 15.7 %all-to-all-start = ((bf16[16,9,8,128]{3,2,1,0:T(8,128)(2,1)}), bf16[16,9,8,128]{3,2,1,0:T(8,128)(2,1)S(1)}, u32[]{:S(2)}, u32[]{:S(2)}) async-start(bf16[16,9,8,128]{3,2,1,0:T(8,128)(2,1)} %fusion.5), calls=%async_computation | async-start | bytes 589824 | tf_op jit(solution)/shard_map/all_to_all | solution.py:22
  18.3 4.7 %collective-permute-start.2 = (bf16[448,512]{1,0:T(8,128)(2,1)}, bf16[448,512]{1,0:T(8,128)(2,1)S(1)}, u32[]{:S(2)}, u32[]{:S(2)}) collective-permute-start(bf16[448,512]{1,0:T(8,128)(2,1)} %bitcast.102), channel_id=1, source_target_pairs={{0,256},{256,0},{1,257},{257,1},{2,258},{258,2},{3,259},{259,3},{4... | collective-permute-start | bytes 1376264 | tf_op jit(solution)/shard_map/ppermute | solution.py:121
  23.0 0.7 broadcast_select_fusion.7
  23.7 4.3 %collective-permute-start = (bf16[16,448]{1,0:T(8,128)(2,1)S(1)}, bf16[16,448]{1,0:T(8,128)(2,1)S(1)}, u32[]{:S(2)}, u32[]{:S(2)}) collective-permute-start(bf16[16,448]{1,0:T(8,128)(2,1)S(1)} %get-tuple-element.22), channel_id=1, source_target_pairs={{0,0},{1,2},{2,4},{3,6},{4,8},{5,10},{6,12},{7,14},{8,256},{9,258}... | collective-permute-start | bytes 43016 | tf_op jit(solution)/shard_map/ppermute | solution.py:124
  28.0 3.9 %collective-permute-start.1 = (bf16[16,448]{1,0:T(8,128)(2,1)S(1)}, bf16[16,448]{1,0:T(8,128)(2,1)S(1)}, u32[]{:S(2)}, u32[]{:S(2)}) collective-permute-start(bf16[16,448]{1,0:T(8,128)(2,1)S(1)} %get-tuple-element.23), channel_id=1, source_target_pairs={{0,1},{1,3},{2,5},{3,7},{4,9},{5,11},{6,13},{7,15},{8,257},{9,259}... | collective-permute-start | bytes 43016 | tf_op jit(solution)/shard_map/ppermute | solution.py:125
  32.0 2.8 %collective-permute-done = bf16[16,448]{1,0:T(8,128)(2,1)S(1)} collective-permute-done((bf16[16,448]{1,0:T(8,128)(2,1)S(1)}, bf16[16,448]{1,0:T(8,128)(2,1)S(1)}, u32[]{:S(2)}, u32[]{:S(2)}) %collective-permute-start) | collective-permute-done | bytes 14368 | tf_op jit(solution)/shard_map/ppermute | solution.py:124
  34.8 0.0 collective-permute-done.1
  34.8 0.1 pad_maximum_fusion.2
  34.9 0.0 all-to-all-done
  34.9 0.0 collective-permute-done.2
  34.9 0.0 copy-done.1
  34.9 0.5 fusion
  35.4 22.9 %all_to_all.20 = f32[16,16,896]{2,1,0:T(8,128)S(1)} all-to-all(f32[16,16,896]{2,1,0:T(8,128)S(1)} %bitcast.96), channel_id=1, replica_groups=mesh['xh'=2,'zq'=8,'zp'=2,'xl'=2,'y'=4,'core'=2] {'xl','y','core'}, dimensions={0} | all-to-all | bytes 1835008 | tf_op jit(solution)/shard_map/all_to_all | solution.py:22
  58.3 0.1 reduce_sum.9
  58.4 0.1 broadcast_select_fusion.5
  58.4 0.1 maximum_bitcast_fusion.3
  58.5 0.7 broadcast_in_dim.33
  59.2 9.5 %all-to-all-start.2 = ((bf16[16,7,8,128]{3,2,1,0:T(8,128)(2,1)}), bf16[16,7,8,128]{3,2,1,0:T(8,128)(2,1)S(1)}, u32[]{:S(2)}, u32[]{:S(2)}) async-start(bf16[16,7,8,128]{3,2,1,0:T(8,128)(2,1)} %bitcast.13), calls=%async_computation.2 | async-start | bytes 458752 | tf_op jit(solution)/shard_map/all_to_all | solution.py:22
  68.7 4.0 %collective-permute-start.3 = (bf16[256,512]{1,0:T(8,128)(2,1)S(1)}, bf16[256,512]{1,0:T(8,128)(2,1)S(1)}, u32[]{:S(2)}, u32[]{:S(2)}) collective-permute-start(bf16[256,512]{1,0:T(8,128)(2,1)S(1)} %bitcast.92), channel_id=1, source_target_pairs={{0,256},{256,0},{1,257},{257,1},{2,258},{258,2},{3,259},{259,3},{4... | collective-permute-start | bytes 786440 | tf_op jit(solution)/shard_map/ppermute | solution.py:144
  72.8 5.7 %collective-permute-done.3 = bf16[256,512]{1,0:T(8,128)(2,1)S(1)} collective-permute-done((bf16[256,512]{1,0:T(8,128)(2,1)S(1)}, bf16[256,512]{1,0:T(8,128)(2,1)S(1)}, u32[]{:S(2)}, u32[]{:S(2)}) %collective-permute-start.3) | collective-permute-done | bytes 262176 | tf_op jit(solution)/shard_map/ppermute | solution.py:144
  78.5 0.1 maximum_bitcast_fusion
  78.6 0.3 copy.16
  78.9 2.4 %all-to-all-done.2 = bf16[16,7,8,128]{3,2,1,0:T(8,128)(2,1)S(1)} async-done(((bf16[16,7,8,128]{3,2,1,0:T(8,128)(2,1)}), bf16[16,7,8,128]{3,2,1,0:T(8,128)(2,1)S(1)}, u32[]{:S(2)}, u32[]{:S(2)}) %all-to-all-start.2) | async-done | bytes 229408 | tf_op jit(solution)/shard_map/all_to_all | solution.py:22
  81.3 0.1 slice_bitcast_fusion.5
  81.4 0.1 slice_bitcast_fusion.7
  81.5 0.1 maximum_bitcast_fusion.1
  81.7 0.1 broadcast_in_dim.36
  81.8 0.1 broadcast_in_dim.34
  81.9 0.2 pad_maximum_fusion
  82.1 35.3 %all_to_all.21 = bf16[64,13,8,128]{3,2,1,0:T(8,128)(2,1)S(1)} all-to-all(bf16[64,13,8,128]{3,2,1,0:T(8,128)(2,1)S(1)} %bitcast.88), channel_id=1, replica_groups=mesh['xh'=2,'zq'=8,'zp'=2,'xl'=2,'y'=4,'core'=2] {'xh','zp','xl','y','co..., dimensions={0} | all-to-all | bytes 3407872 | tf_op jit(solution)/shard_map/all_to_all | solution.py:22
  117.5 0.1 slice_bitcast_fusion.panel_ref
  117.6 1.8 %shard_map.50 = (f32[448,896]{1,0:T(8,128)}, f32[256,512]{1,0:T(8,128)}) custom-call(bf16[512,512]{1,0:T(8,128)(2,1)S(1)} %slice_bitcast_fusion.1.rows_ref, bf16[512,896]{1,0:T(8,128)(2,1)S(1)} %slice_bitcast_fusion.panel_ref, bf16[2,2,256,128]{3,2,1,0:T(8,128)(2,1)S(1)} %bitcast.87, bf16[512,512]{1,0:T(8,128)(2,1)S(1)} %bitcast.86), custom_call_target="tpu_custom_call" | custom-call | tf_op jit(solution)/shard_map/pallas_call | solution.py:58
  (16 shorter events, 0.3 us)
Async XLA Ops:
  0.6 1.0 copy-start
  0.6 34.3 %copy-start.1 = (bf16[512,448]{0,1:T(8,128)(2,1)S(1)}, bf16[512,448]{0,1:T(8,128)(2,1)}, u32[]{:S(2)}) copy-start(bf16[512,448]{0,1:T(8,128)(2,1)} %param.4) | copy-start | bytes 1376260
  2.5 32.3 %all-to-all-start = ((bf16[16,9,8,128]{3,2,1,0:T(8,128)(2,1)}), bf16[16,9,8,128]{3,2,1,0:T(8,128)(2,1)S(1)}, u32[]{:S(2)}, u32[]{:S(2)}) async-start(bf16[16,9,8,128]{3,2,1,0:T(8,128)(2,1)} %fusion.5), calls=%async_computation | async-start | bytes 589824 | tf_op jit(solution)/shard_map/all_to_all | solution.py:22
  18.3 16.6 %collective-permute-start.2 = (bf16[448,512]{1,0:T(8,128)(2,1)}, bf16[448,512]{1,0:T(8,128)(2,1)S(1)}, u32[]{:S(2)}, u32[]{:S(2)}) collective-permute-start(bf16[448,512]{1,0:T(8,128)(2,1)} %bitcast.102), channel_id=1, source_target_pairs={{0,256},{256,0},{1,257},{257,1},{2,258},{258,2},{3,259},{259,3},{4... | collective-permute-start | bytes 1376264 | tf_op jit(solution)/shard_map/ppermute | solution.py:121
  23.7 11.1 %collective-permute-start = (bf16[16,448]{1,0:T(8,128)(2,1)S(1)}, bf16[16,448]{1,0:T(8,128)(2,1)S(1)}, u32[]{:S(2)}, u32[]{:S(2)}) collective-permute-start(bf16[16,448]{1,0:T(8,128)(2,1)S(1)} %get-tuple-element.22), channel_id=1, source_target_pairs={{0,0},{1,2},{2,4},{3,6},{4,8},{5,10},{6,12},{7,14},{8,256},{9,258}... | collective-permute-start | bytes 43016 | tf_op jit(solution)/shard_map/ppermute | solution.py:124
  28.0 6.8 %collective-permute-start.1 = (bf16[16,448]{1,0:T(8,128)(2,1)S(1)}, bf16[16,448]{1,0:T(8,128)(2,1)S(1)}, u32[]{:S(2)}, u32[]{:S(2)}) collective-permute-start(bf16[16,448]{1,0:T(8,128)(2,1)S(1)} %get-tuple-element.23), channel_id=1, source_target_pairs={{0,1},{1,3},{2,5},{3,7},{4,9},{5,11},{6,13},{7,15},{8,257},{9,259}... | collective-permute-start | bytes 43016 | tf_op jit(solution)/shard_map/ppermute | solution.py:125
  59.2 22.1 %all-to-all-start.2 = ((bf16[16,7,8,128]{3,2,1,0:T(8,128)(2,1)}), bf16[16,7,8,128]{3,2,1,0:T(8,128)(2,1)S(1)}, u32[]{:S(2)}, u32[]{:S(2)}) async-start(bf16[16,7,8,128]{3,2,1,0:T(8,128)(2,1)} %bitcast.13), calls=%async_computation.2 | async-start | bytes 458752 | tf_op jit(solution)/shard_map/all_to_all | solution.py:22
  68.7 9.7 %collective-permute-start.3 = (bf16[256,512]{1,0:T(8,128)(2,1)S(1)}, bf16[256,512]{1,0:T(8,128)(2,1)S(1)}, u32[]{:S(2)}, u32[]{:S(2)}) collective-permute-start(bf16[256,512]{1,0:T(8,128)(2,1)S(1)} %bitcast.92), channel_id=1, source_target_pairs={{0,256},{256,0},{1,257},{257,1},{2,258},{258,2},{3,259},{259,3},{4... | collective-permute-start | bytes 786440 | tf_op jit(solution)/shard_map/ppermute | solution.py:144

commit v9 on v7

--- a/solution.py
+++ b/solution.py
@@ -32,14 +32,8 @@
 
 
 def covariance_kernel(scale, rows_ref, panel_ref, act_rows_ref, cols_ref, grad_ref, act_ref, grad, act, act_t, sems):
-    nx, halves, count, width = act_rows_ref.shape
-    for x in range(nx):
-        for h in range(halves):
-            act_t[h * width : (h + 1) * width, x * count : (x + 1) * count] = act_rows_ref[x, h].T
-    act[...] = jnp.dot(act_t[...], cols_ref[...], preferred_element_type=jnp.float32) * scale
-    copies = [pltpu.make_async_copy(act, act_ref, sems.at[0])]
-    copies[0].start()
     steps, height, _ = grad.shape
+    copies = []
     rows_t = rows_ref[...].T
     for k in range(steps):
         mine = rows_t[k * height : (k + 1) * height]
@@ -47,6 +41,13 @@
         copy = pltpu.make_async_copy(grad.at[k], grad_ref.at[pl.ds(k * height, height)], sems.at[1 + k])
         copy.start()
         copies.append(copy)
+    nx, halves, count, width = act_rows_ref.shape
+    for x in range(nx):
+        for h in range(halves):
+            act_t[h * width : (h + 1) * width, x * count : (x + 1) * count] = act_rows_ref[x, h].T
+    act[...] = jnp.dot(act_t[...], cols_ref[...], preferred_element_type=jnp.float32) * scale
+    copies.append(pltpu.make_async_copy(act, act_ref, sems.at[0]))
+    copies[-1].start()
     for copy in copies:
         copy.wait()
 

time: 115 us -> 115 us (level)
  no operation moved by 1% of the time
where the time goes in v9:
time: 115 us; the launch traced here: 114 us
  blocking collectives  53.2 us (46%)
  starting transfers between devices  42.1 us (37%)
  waiting for transfers between devices  11 us (10%)
  local copies, waits for them, and re-layouts  2.72 us (2%)
  other arithmetic  2.27 us (2%)
  Pallas kernels  1.78 us (2%)
    all_to_all x2, blocking collectives, exchange(): return lax.all_to_all(parts, axis, split_axis=0, concat_axis=0, tiled=True)  53.2 us
    all_to_all x2, starting transfers between devices, exchange(): return lax.all_to_all(parts, axis, split_axis=0, concat_axis=0, tiled=True)  25.2 us
    ppermute x1, waiting for transfers between devices, shards(): other_half = lax.ppermute(half, 'xh', swap)  5.72 us
    ppermute x1, starting transfers between devices, shards(): other_weight = lax.ppermute(own_weight, 'xh', swap)  4.65 us
    ppermute x1, starting transfers between devices, shards(): lax.ppermute(jnp.where(xh == 0, halves[0], halves[1]), LEVEL, moves(0))  4.31 us
    ppermute x1, starting transfers between devices, shards(): other_half = lax.ppermute(half, 'xh', swap)  3.99 us
    ppermute x1, starting transfers between devices, shards(): lax.ppermute(jnp.where(xh == 0, halves[1], halves[0]), LEVEL, moves(1))  3.92 us
    ppermute x1, waiting for transfers between devices, shards(): lax.ppermute(jnp.where(xh == 0, halves[0], halves[1]), LEVEL, moves(0))  2.83 us
  transfers between devices with their start and end apart: 6, of which 3 were waited for; matrix products, arithmetic and copies ran while one was open for 1% of the time, Pallas kernels for 0%

profile of v9, /device:TPU:1, one launch (start us, length us, event | category | flops | bytes accessed | tf_op | source)
XLA Modules:
  0.0 114.5 jit_solution(613421402059295788)
XLA Ops:
  0.6 0.0 copy-start
  0.6 0.0 copy-start.1
  0.7 0.9 copy-done
  1.6 0.1 dynamic-slice_reduce_fusion
  1.8 0.7 fusion.4
  2.5 15.7 %all-to-all-start = ((bf16[16,9,8,128]{3,2,1,0:T(8,128)(2,1)}), bf16[16,9,8,128]{3,2,1,0:T(8,128)(2,1)S(1)}, u32[]{:S(2)}, u32[]{:S(2)}) async-start(bf16[16,9,8,128]{3,2,1,0:T(8,128)(2,1)} %fusion.4), calls=%async_computation | async-start | bytes 589824 | tf_op jit(solution)/shard_map/all_to_all | solution.py:22
  18.3 4.7 %collective-permute-start.2 = (bf16[448,512]{1,0:T(8,128)(2,1)}, bf16[448,512]{1,0:T(8,128)(2,1)S(1)}, u32[]{:S(2)}, u32[]{:S(2)}) collective-permute-start(bf16[448,512]{1,0:T(8,128)(2,1)} %bitcast.102), channel_id=1, source_target_pairs={{0,256},{256,0},{1,257},{257,1},{2,258},{258,2},{3,259},{259,3},{4... | collective-permute-start | bytes 1376264 | tf_op jit(solution)/shard_map/ppermute | solution.py:122
  23.0 0.7 broadcast_select_fusion.7
  23.7 4.3 %collective-permute-start = (bf16[16,448]{1,0:T(8,128)(2,1)S(1)}, bf16[16,448]{1,0:T(8,128)(2,1)S(1)}, u32[]{:S(2)}, u32[]{:S(2)}) collective-permute-start(bf16[16,448]{1,0:T(8,128)(2,1)S(1)} %get-tuple-element.22), channel_id=1, source_target_pairs={{0,0},{1,2},{2,4},{3,6},{4,8},{5,10},{6,12},{7,14},{8,256},{9,258}... | collective-permute-start | bytes 43016 | tf_op jit(solution)/shard_map/ppermute | solution.py:125
  28.0 3.9 %collective-permute-start.1 = (bf16[16,448]{1,0:T(8,128)(2,1)S(1)}, bf16[16,448]{1,0:T(8,128)(2,1)S(1)}, u32[]{:S(2)}, u32[]{:S(2)}) collective-permute-start(bf16[16,448]{1,0:T(8,128)(2,1)S(1)} %get-tuple-element.23), channel_id=1, source_target_pairs={{0,1},{1,3},{2,5},{3,7},{4,9},{5,11},{6,13},{7,15},{8,257},{9,259}... | collective-permute-start | bytes 43016 | tf_op jit(solution)/shard_map/ppermute | solution.py:126
  32.0 2.8 %collective-permute-done = bf16[16,448]{1,0:T(8,128)(2,1)S(1)} collective-permute-done((bf16[16,448]{1,0:T(8,128)(2,1)S(1)}, bf16[16,448]{1,0:T(8,128)(2,1)S(1)}, u32[]{:S(2)}, u32[]{:S(2)}) %collective-permute-start) | collective-permute-done | bytes 14368 | tf_op jit(solution)/shard_map/ppermute | solution.py:125
  34.8 0.0 collective-permute-done.1
  34.8 0.1 pad_maximum_fusion.2
  34.9 0.0 all-to-all-done
  34.9 0.0 collective-permute-done.2
  34.9 0.0 copy-done.1
  34.9 0.5 convolution_convert_fusion
  35.4 17.9 %all_to_all.20 = bf16[16,16,896]{2,1,0:T(8,128)(2,1)S(1)} all-to-all(bf16[16,16,896]{2,1,0:T(8,128)(2,1)S(1)} %bitcast.97), channel_id=1, replica_groups=mesh['xh'=2,'zq'=8,'zp'=2,'xl'=2,'y'=4,'core'=2] {'xl','y','core'}, dimensions={0} | all-to-all | bytes 917504 | tf_op jit(solution)/shard_map/all_to_all | solution.py:22
  53.3 0.1 convert_reduce_fusion
  53.5 0.1 broadcast_select_fusion.5
  53.5 0.1 maximum_bitcast_fusion.3
  53.6 0.7 broadcast_in_dim.33
  54.3 9.5 %all-to-all-start.2 = ((bf16[16,7,8,128]{3,2,1,0:T(8,128)(2,1)}), bf16[16,7,8,128]{3,2,1,0:T(8,128)(2,1)S(1)}, u32[]{:S(2)}, u32[]{:S(2)}) async-start(bf16[16,7,8,128]{3,2,1,0:T(8,128)(2,1)} %bitcast.13), calls=%async_computation.2 | async-start | bytes 458752 | tf_op jit(solution)/shard_map/all_to_all | solution.py:22
  63.8 4.0 %collective-permute-start.3 = (bf16[256,512]{1,0:T(8,128)(2,1)S(1)}, bf16[256,512]{1,0:T(8,128)(2,1)S(1)}, u32[]{:S(2)}, u32[]{:S(2)}) collective-permute-start(bf16[256,512]{1,0:T(8,128)(2,1)S(1)} %bitcast.92), channel_id=1, source_target_pairs={{0,256},{256,0},{1,257},{257,1},{2,258},{258,2},{3,259},{259,3},{4... | collective-permute-start | bytes 786440 | tf_op jit(solution)/shard_map/ppermute | solution.py:145
  67.8 5.7 %collective-permute-done.3 = bf16[256,512]{1,0:T(8,128)(2,1)S(1)} collective-permute-done((bf16[256,512]{1,0:T(8,128)(2,1)S(1)}, bf16[256,512]{1,0:T(8,128)(2,1)S(1)}, u32[]{:S(2)}, u32[]{:S(2)}) %collective-permute-start.3) | collective-permute-done | bytes 262176 | tf_op jit(solution)/shard_map/ppermute | solution.py:145
  73.6 0.1 maximum_bitcast_fusion
  73.7 0.3 copy.16
  74.0 2.4 %all-to-all-done.2 = bf16[16,7,8,128]{3,2,1,0:T(8,128)(2,1)S(1)} async-done(((bf16[16,7,8,128]{3,2,1,0:T(8,128)(2,1)}), bf16[16,7,8,128]{3,2,1,0:T(8,128)(2,1)S(1)}, u32[]{:S(2)}, u32[]{:S(2)}) %all-to-all-start.2) | async-done | bytes 229408 | tf_op jit(solution)/shard_map/all_to_all | solution.py:22
  76.4 0.1 slice_bitcast_fusion.5
  76.5 0.1 slice_bitcast_fusion.7
  76.6 0.1 maximum_bitcast_fusion.1
  76.8 0.1 broadcast_in_dim.36
  76.9 0.1 broadcast_in_dim.34
  77.0 0.2 pad_maximum_fusion
  77.2 35.3 %all_to_all.21 = bf16[64,13,8,128]{3,2,1,0:T(8,128)(2,1)S(1)} all-to-all(bf16[64,13,8,128]{3,2,1,0:T(8,128)(2,1)S(1)} %bitcast.88), channel_id=1, replica_groups=mesh['xh'=2,'zq'=8,'zp'=2,'xl'=2,'y'=4,'core'=2] {'xh','zp','xl','y','co..., dimensions={0} | all-to-all | bytes 3407872 | tf_op jit(solution)/shard_map/all_to_all | solution.py:22
  112.6 0.1 slice_bitcast_fusion.panel_ref
  112.7 1.8 %shard_map.50 = (f32[448,896]{1,0:T(8,128)}, f32[256,512]{1,0:T(8,128)}) custom-call(bf16[512,512]{1,0:T(8,128)(2,1)S(1)} %slice_bitcast_fusion.1.rows_ref, bf16[512,896]{1,0:T(8,128)(2,1)S(1)} %slice_bitcast_fusion.panel_ref, bf16[2,2,256,128]{3,2,1,0:T(8,128)(2,1)S(1)} %bitcast.87, bf16[512,512]{1,0:T(8,128)(2,1)S(1)} %bitcast.86), custom_call_target="tpu_custom_call" | custom-call | tf_op jit(solution)/shard_map/pallas_call | solution.py:59
  (16 shorter events, 0.3 us)
Async XLA Ops:
  0.6 1.0 copy-start
  0.6 34.3 %copy-start.1 = (bf16[512,448]{0,1:T(8,128)(2,1)S(1)}, bf16[512,448]{0,1:T(8,128)(2,1)}, u32[]{:S(2)}) copy-start(bf16[512,448]{0,1:T(8,128)(2,1)} %param.4) | copy-start | bytes 1376260
  2.5 32.3 %all-to-all-start = ((bf16[16,9,8,128]{3,2,1,0:T(8,128)(2,1)}), bf16[16,9,8,128]{3,2,1,0:T(8,128)(2,1)S(1)}, u32[]{:S(2)}, u32[]{:S(2)}) async-start(bf16[16,9,8,128]{3,2,1,0:T(8,128)(2,1)} %fusion.4), calls=%async_computation | async-start | bytes 589824 | tf_op jit(solution)/shard_map/all_to_all | solution.py:22
  18.3 16.6 %collective-permute-start.2 = (bf16[448,512]{1,0:T(8,128)(2,1)}, bf16[448,512]{1,0:T(8,128)(2,1)S(1)}, u32[]{:S(2)}, u32[]{:S(2)}) collective-permute-start(bf16[448,512]{1,0:T(8,128)(2,1)} %bitcast.102), channel_id=1, source_target_pairs={{0,256},{256,0},{1,257},{257,1},{2,258},{258,2},{3,259},{259,3},{4... | collective-permute-start | bytes 1376264 | tf_op jit(solution)/shard_map/ppermute | solution.py:122
  23.7 11.1 %collective-permute-start = (bf16[16,448]{1,0:T(8,128)(2,1)S(1)}, bf16[16,448]{1,0:T(8,128)(2,1)S(1)}, u32[]{:S(2)}, u32[]{:S(2)}) collective-permute-start(bf16[16,448]{1,0:T(8,128)(2,1)S(1)} %get-tuple-element.22), channel_id=1, source_target_pairs={{0,0},{1,2},{2,4},{3,6},{4,8},{5,10},{6,12},{7,14},{8,256},{9,258}... | collective-permute-start | bytes 43016 | tf_op jit(solution)/shard_map/ppermute | solution.py:125
  28.0 6.8 %collective-permute-start.1 = (bf16[16,448]{1,0:T(8,128)(2,1)S(1)}, bf16[16,448]{1,0:T(8,128)(2,1)S(1)}, u32[]{:S(2)}, u32[]{:S(2)}) collective-permute-start(bf16[16,448]{1,0:T(8,128)(2,1)S(1)} %get-tuple-element.23), channel_id=1, source_target_pairs={{0,1},{1,3},{2,5},{3,7},{4,9},{5,11},{6,13},{7,15},{8,257},{9,259}... | collective-permute-start | bytes 43016 | tf_op jit(solution)/shard_map/ppermute | solution.py:126
  54.3 22.1 %all-to-all-start.2 = ((bf16[16,7,8,128]{3,2,1,0:T(8,128)(2,1)}), bf16[16,7,8,128]{3,2,1,0:T(8,128)(2,1)S(1)}, u32[]{:S(2)}, u32[]{:S(2)}) async-start(bf16[16,7,8,128]{3,2,1,0:T(8,128)(2,1)} %bitcast.13), calls=%async_computation.2 | async-start | bytes 458752 | tf_op jit(solution)/shard_map/all_to_all | solution.py:22
  63.8 9.7 %collective-permute-start.3 = (bf16[256,512]{1,0:T(8,128)(2,1)S(1)}, bf16[256,512]{1,0:T(8,128)(2,1)S(1)}, u32[]{:S(2)}, u32[]{:S(2)}) collective-permute-start(bf16[256,512]{1,0:T(8,128)(2,1)S(1)} %bitcast.92), channel_id=1, source_target_pairs={{0,256},{256,0},{1,257},{257,1},{2,258},{258,2},{3,259},{259,3},{4... | collective-permute-start | bytes 786440 | tf_op jit(solution)/shard_map/ppermute | solution.py:145

commit v10 on v9

--- a/solution.py
+++ b/solution.py
@@ -53,7 +53,7 @@
 
 
 def covariances(rows, panel, act_rows, cols, height, scale):
-    steps = 2
+    steps = 1
     grad_shape = (height, panel.shape[1])
     act_shape = (act_rows.shape[1] * act_rows.shape[3], cols.shape[1])
     return pl.pallas_call(

time: 115 us -> 115 us (level)
  no operation moved by 1% of the time
where the time goes in v10:
time: 115 us
  blocking collectives  53.2 us (46%)
  starting transfers between devices  42.1 us (37%)
  waiting for transfers between devices  11 us (10%)
  local copies, waits for them, and re-layouts  2.72 us (2%)
  other arithmetic  2.27 us (2%)
  Pallas kernels  2.02 us (2%)
    all_to_all x2, blocking collectives, exchange(): return lax.all_to_all(parts, axis, split_axis=0, concat_axis=0, tiled=True)  53.2 us
    all_to_all x2, starting transfers between devices, exchange(): return lax.all_to_all(parts, axis, split_axis=0, concat_axis=0, tiled=True)  25.2 us
    ppermute x1, waiting for transfers between devices, shards(): other_half = lax.ppermute(half, 'xh', swap)  5.72 us
    ppermute x1, starting transfers between devices, shards(): other_weight = lax.ppermute(own_weight, 'xh', swap)  4.65 us
    ppermute x1, starting transfers between devices, shards(): lax.ppermute(jnp.where(xh == 0, halves[0], halves[1]), LEVEL, moves(0))  4.31 us
    ppermute x1, starting transfers between devices, shards(): other_half = lax.ppermute(half, 'xh', swap)  3.99 us
    ppermute x1, starting transfers between devices, shards(): lax.ppermute(jnp.where(xh == 0, halves[1], halves[0]), LEVEL, moves(1))  3.92 us
    ppermute x1, waiting for transfers between devices, shards(): lax.ppermute(jnp.where(xh == 0, halves[0], halves[1]), LEVEL, moves(0))  2.83 us
  transfers between devices with their start and end apart: 6, of which 3 were waited for; matrix products, arithmetic and copies ran while one was open for 1% of the time, Pallas kernels for 0%

profile of v10, /device:TPU:1, one launch (start us, length us, event | category | flops | bytes accessed | tf_op | source)
XLA Modules:
  0.0 114.7 jit_solution(17383581576050394888)
XLA Ops:
  0.6 0.0 copy-start
  0.6 0.0 copy-start.1
  0.7 0.9 copy-done
  1.6 0.1 dynamic-slice_reduce_fusion
  1.8 0.7 fusion.4
  2.5 15.7 %all-to-all-start = ((bf16[16,9,8,128]{3,2,1,0:T(8,128)(2,1)}), bf16[16,9,8,128]{3,2,1,0:T(8,128)(2,1)S(1)}, u32[]{:S(2)}, u32[]{:S(2)}) async-start(bf16[16,9,8,128]{3,2,1,0:T(8,128)(2,1)} %fusion.4), calls=%async_computation | async-start | bytes 589824 | tf_op jit(solution)/shard_map/all_to_all | solution.py:22
  18.3 4.7 %collective-permute-start.2 = (bf16[448,512]{1,0:T(8,128)(2,1)}, bf16[448,512]{1,0:T(8,128)(2,1)S(1)}, u32[]{:S(2)}, u32[]{:S(2)}) collective-permute-start(bf16[448,512]{1,0:T(8,128)(2,1)} %bitcast.102), channel_id=1, source_target_pairs={{0,256},{256,0},{1,257},{257,1},{2,258},{258,2},{3,259},{259,3},{4... | collective-permute-start | bytes 1376264 | tf_op jit(solution)/shard_map/ppermute | solution.py:122
  23.0 0.7 broadcast_select_fusion.7
  23.7 4.3 %collective-permute-start = (bf16[16,448]{1,0:T(8,128)(2,1)S(1)}, bf16[16,448]{1,0:T(8,128)(2,1)S(1)}, u32[]{:S(2)}, u32[]{:S(2)}) collective-permute-start(bf16[16,448]{1,0:T(8,128)(2,1)S(1)} %get-tuple-element.22), channel_id=1, source_target_pairs={{0,0},{1,2},{2,4},{3,6},{4,8},{5,10},{6,12},{7,14},{8,256},{9,258}... | collective-permute-start | bytes 43016 | tf_op jit(solution)/shard_map/ppermute | solution.py:125
  28.0 3.9 %collective-permute-start.1 = (bf16[16,448]{1,0:T(8,128)(2,1)S(1)}, bf16[16,448]{1,0:T(8,128)(2,1)S(1)}, u32[]{:S(2)}, u32[]{:S(2)}) collective-permute-start(bf16[16,448]{1,0:T(8,128)(2,1)S(1)} %get-tuple-element.23), channel_id=1, source_target_pairs={{0,1},{1,3},{2,5},{3,7},{4,9},{5,11},{6,13},{7,15},{8,257},{9,259}... | collective-permute-start | bytes 43016 | tf_op jit(solution)/shard_map/ppermute | solution.py:126
  32.0 2.8 %collective-permute-done = bf16[16,448]{1,0:T(8,128)(2,1)S(1)} collective-permute-done((bf16[16,448]{1,0:T(8,128)(2,1)S(1)}, bf16[16,448]{1,0:T(8,128)(2,1)S(1)}, u32[]{:S(2)}, u32[]{:S(2)}) %collective-permute-start) | collective-permute-done | bytes 14368 | tf_op jit(solution)/shard_map/ppermute | solution.py:125
  34.8 0.0 collective-permute-done.1
  34.8 0.1 pad_maximum_fusion.2
  34.9 0.0 all-to-all-done
  34.9 0.0 collective-permute-done.2
  34.9 0.0 copy-done.1
  34.9 0.5 convolution_convert_fusion
  35.4 17.9 %all_to_all.20 = bf16[16,16,896]{2,1,0:T(8,128)(2,1)S(1)} all-to-all(bf16[16,16,896]{2,1,0:T(8,128)(2,1)S(1)} %bitcast.97), channel_id=1, replica_groups=mesh['xh'=2,'zq'=8,'zp'=2,'xl'=2,'y'=4,'core'=2] {'xl','y','core'}, dimensions={0} | all-to-all | bytes 917504 | tf_op jit(solution)/shard_map/all_to_all | solution.py:22
  53.3 0.1 convert_reduce_fusion
  53.5 0.1 broadcast_select_fusion.5
  53.5 0.1 maximum_bitcast_fusion.3
  53.6 0.7 broadcast_in_dim.33
  54.3 9.5 %all-to-all-start.2 = ((bf16[16,7,8,128]{3,2,1,0:T(8,128)(2,1)}), bf16[16,7,8,128]{3,2,1,0:T(8,128)(2,1)S(1)}, u32[]{:S(2)}, u32[]{:S(2)}) async-start(bf16[16,7,8,128]{3,2,1,0:T(8,128)(2,1)} %bitcast.13), calls=%async_computation.2 | async-start | bytes 458752 | tf_op jit(solution)/shard_map/all_to_all | solution.py:22
  63.8 4.0 %collective-permute-start.3 = (bf16[256,512]{1,0:T(8,128)(2,1)S(1)}, bf16[256,512]{1,0:T(8,128)(2,1)S(1)}, u32[]{:S(2)}, u32[]{:S(2)}) collective-permute-start(bf16[256,512]{1,0:T(8,128)(2,1)S(1)} %bitcast.92), channel_id=1, source_target_pairs={{0,256},{256,0},{1,257},{257,1},{2,258},{258,2},{3,259},{259,3},{4... | collective-permute-start | bytes 786440 | tf_op jit(solution)/shard_map/ppermute | solution.py:145
  67.8 5.7 %collective-permute-done.3 = bf16[256,512]{1,0:T(8,128)(2,1)S(1)} collective-permute-done((bf16[256,512]{1,0:T(8,128)(2,1)S(1)}, bf16[256,512]{1,0:T(8,128)(2,1)S(1)}, u32[]{:S(2)}, u32[]{:S(2)}) %collective-permute-start.3) | collective-permute-done | bytes 262176 | tf_op jit(solution)/shard_map/ppermute | solution.py:145
  73.6 0.1 maximum_bitcast_fusion
  73.7 0.3 copy.16
  74.0 2.4 %all-to-all-done.2 = bf16[16,7,8,128]{3,2,1,0:T(8,128)(2,1)S(1)} async-done(((bf16[16,7,8,128]{3,2,1,0:T(8,128)(2,1)}), bf16[16,7,8,128]{3,2,1,0:T(8,128)(2,1)S(1)}, u32[]{:S(2)}, u32[]{:S(2)}) %all-to-all-start.2) | async-done | bytes 229408 | tf_op jit(solution)/shard_map/all_to_all | solution.py:22
  76.4 0.1 slice_bitcast_fusion.5
  76.5 0.1 slice_bitcast_fusion.7
  76.6 0.1 maximum_bitcast_fusion.1
  76.8 0.1 broadcast_in_dim.36
  76.9 0.1 broadcast_in_dim.34
  77.0 0.2 pad_maximum_fusion
  77.2 35.3 %all_to_all.21 = bf16[64,13,8,128]{3,2,1,0:T(8,128)(2,1)S(1)} all-to-all(bf16[64,13,8,128]{3,2,1,0:T(8,128)(2,1)S(1)} %bitcast.88), channel_id=1, replica_groups=mesh['xh'=2,'zq'=8,'zp'=2,'xl'=2,'y'=4,'core'=2] {'xh','zp','xl','y','co..., dimensions={0} | all-to-all | bytes 3407872 | tf_op jit(solution)/shard_map/all_to_all | solution.py:22
  112.6 0.1 slice_bitcast_fusion.panel_ref
  112.7 2.0 %shard_map.50 = (f32[448,896]{1,0:T(8,128)}, f32[256,512]{1,0:T(8,128)}) custom-call(bf16[512,512]{1,0:T(8,128)(2,1)S(1)} %slice_bitcast_fusion.1.rows_ref, bf16[512,896]{1,0:T(8,128)(2,1)S(1)} %slice_bitcast_fusion.panel_ref, bf16[2,2,256,128]{3,2,1,0:T(8,128)(2,1)S(1)} %bitcast.87, bf16[512,512]{1,0:T(8,128)(2,1)S(1)} %bitcast.86), custom_call_target="tpu_custom_call" | custom-call | tf_op jit(solution)/shard_map/pallas_call | solution.py:59
  (16 shorter events, 0.3 us)
Async XLA Ops:
  0.6 1.0 copy-start
  0.6 34.3 %copy-start.1 = (bf16[512,448]{0,1:T(8,128)(2,1)S(1)}, bf16[512,448]{0,1:T(8,128)(2,1)}, u32[]{:S(2)}) copy-start(bf16[512,448]{0,1:T(8,128)(2,1)} %param.4) | copy-start | bytes 1376260
  2.5 32.3 %all-to-all-start = ((bf16[16,9,8,128]{3,2,1,0:T(8,128)(2,1)}), bf16[16,9,8,128]{3,2,1,0:T(8,128)(2,1)S(1)}, u32[]{:S(2)}, u32[]{:S(2)}) async-start(bf16[16,9,8,128]{3,2,1,0:T(8,128)(2,1)} %fusion.4), calls=%async_computation | async-start | bytes 589824 | tf_op jit(solution)/shard_map/all_to_all | solution.py:22
  18.3 16.6 %collective-permute-start.2 = (bf16[448,512]{1,0:T(8,128)(2,1)}, bf16[448,512]{1,0:T(8,128)(2,1)S(1)}, u32[]{:S(2)}, u32[]{:S(2)}) collective-permute-start(bf16[448,512]{1,0:T(8,128)(2,1)} %bitcast.102), channel_id=1, source_target_pairs={{0,256},{256,0},{1,257},{257,1},{2,258},{258,2},{3,259},{259,3},{4... | collective-permute-start | bytes 1376264 | tf_op jit(solution)/shard_map/ppermute | solution.py:122
  23.7 11.1 %collective-permute-start = (bf16[16,448]{1,0:T(8,128)(2,1)S(1)}, bf16[16,448]{1,0:T(8,128)(2,1)S(1)}, u32[]{:S(2)}, u32[]{:S(2)}) collective-permute-start(bf16[16,448]{1,0:T(8,128)(2,1)S(1)} %get-tuple-element.22), channel_id=1, source_target_pairs={{0,0},{1,2},{2,4},{3,6},{4,8},{5,10},{6,12},{7,14},{8,256},{9,258}... | collective-permute-start | bytes 43016 | tf_op jit(solution)/shard_map/ppermute | solution.py:125
  28.0 6.8 %collective-permute-start.1 = (bf16[16,448]{1,0:T(8,128)(2,1)S(1)}, bf16[16,448]{1,0:T(8,128)(2,1)S(1)}, u32[]{:S(2)}, u32[]{:S(2)}) collective-permute-start(bf16[16,448]{1,0:T(8,128)(2,1)S(1)} %get-tuple-element.23), channel_id=1, source_target_pairs={{0,1},{1,3},{2,5},{3,7},{4,9},{5,11},{6,13},{7,15},{8,257},{9,259}... | collective-permute-start | bytes 43016 | tf_op jit(solution)/shard_map/ppermute | solution.py:126
  54.3 22.1 %all-to-all-start.2 = ((bf16[16,7,8,128]{3,2,1,0:T(8,128)(2,1)}), bf16[16,7,8,128]{3,2,1,0:T(8,128)(2,1)S(1)}, u32[]{:S(2)}, u32[]{:S(2)}) async-start(bf16[16,7,8,128]{3,2,1,0:T(8,128)(2,1)} %bitcast.13), calls=%async_computation.2 | async-start | bytes 458752 | tf_op jit(solution)/shard_map/all_to_all | solution.py:22
  63.8 9.7 %collective-permute-start.3 = (bf16[256,512]{1,0:T(8,128)(2,1)S(1)}, bf16[256,512]{1,0:T(8,128)(2,1)S(1)}, u32[]{:S(2)}, u32[]{:S(2)}) collective-permute-start(bf16[256,512]{1,0:T(8,128)(2,1)S(1)} %bitcast.92), channel_id=1, source_target_pairs={{0,256},{256,0},{1,257},{257,1},{2,258},{258,2},{3,259},{259,3},{4... | collective-permute-start | bytes 786440 | tf_op jit(solution)/shard_map/ppermute | solution.py:145
